TPU v7x, 128 devices: a whole 4x4x4 slice. The times are simulated.
128 devices in a mesh: flow: 32 (over y, z, core), grp: 4 (over x).
Axes of the slice: x: 4, y: 4, z: 4, core: 2. Of those that a mesh axis runs over, the one named last changes fastest.
Arguments:
- fluid_point_warmth: float32 [512, 131072], P(None, ('flow', 'grp')), may hold values from -6 to 6
- velocity: float32 [512, 131072], P(None, ('flow', 'grp')), may hold values from 0.3 to 1.2
- wall_film: float32 [128, 131072], P(None, ('flow', 'grp')), may hold values from 0.5 to 5
- face_owner: int32 [262144, 1], P(('flow', 'grp')), may hold values from 0 to 127; in each aligned block of 2048 rows (0 to 2047, 2048 to 4095, ...) at most 32 rows name the same one
- plate_temp: float32 [128, 65536], P(None, ('flow', 'grp')), may hold values from -6 to 6
- conductivity: float32 [128, 65536], P(None, ('flow', 'grp')), may hold values from 0.25 to 2
- plate_cell: int32 [524288], P(('flow', 'grp')), may hold values from 0 to 511
Outputs:
- coolant_out: float32 [512, 131072], P(None, ('flow', 'grp'))
- boundary_sheet_warmth: float32 [128, 131072], P(None, ('flow', 'grp'))
- sheet_conducted_warmth: float32 [128, 65536], P(None, ('flow', 'grp'))
Inputs may be any that keep to these rules, and one draw needn't show every extreme that they name: `face_owner`: among the 2048 faces of one device at most 32 name the same owner, and that bound is reached.
All inputs are finite; a program needn't handle non-finite values.
Results may differ from a plain program's by a relative error of at most 0.0001.
Values sent between devices are 32-bit elements; how exact they have to be, the bound alone decides.
No kernel may reach another device: no remote copies, remote signals or barrier semaphores. Data moves between devices by JAX's collectives and lax.ppermute only.
A program may use at most 64 MiB of HBM per device.

v0:
```python
import functools

import jax
import jax.numpy as jnp
import ml_dtypes
import numpy as np
from jax import lax
from jax.experimental import pallas as pl
from jax.experimental.pallas import tpu as pltpu
from jax.sharding import PartitionSpec as P

SWEEPS = 2
LAMBDA_H = 4.0
DAMPING_RATIO = 0.5
CARRY_STEP_SIZE = 0.05
CONTACT = 0.1
DT_PLATE = 0.0008
COUPLE = 20.0
MIXING_WEIGHT = 0.5
GLL_POINTS = (
    -1.0,
    -0.8717401485096066,
    -0.5917001814331423,
    -0.2092992179024789,
    0.2092992179024789,
    0.5917001814331423,
    0.8717401485096066,
    1.0,
)
GLL_WEIGHTS = (
    0.03571428571428571,
    0.2107042271435061,
    0.3411226924835044,
    0.4124587946587038,
    0.4124587946587038,
    0.3411226924835044,
    0.2107042271435061,
    0.03571428571428571,
)
LANES = 128
VMEM_LIMIT = 56 * 1024 * 1024


def split_pair(table):
    high = np.asarray(table, np.float32).astype(ml_dtypes.bfloat16)
    low = (np.asarray(table, np.float64) - high.astype(np.float64)).astype(np.float32)
    return high, low.astype(ml_dtypes.bfloat16)


def gll_tables():
    points = np.array(GLL_POINTS)
    weights = np.array(GLL_WEIGHTS)
    identity = np.eye(8)
    spread = points[:, None] - points[None, :] + identity
    bary_weight = 1.0 / np.prod(spread, axis=1)
    gradient = bary_weight[None, :] / bary_weight[:, None] / spread
    gradient = gradient * (1.0 - identity)
    gradient = gradient - identity * gradient.sum(axis=1)[:, None]
    stiffness = gradient.T * weights[None, :] @ gradient
    strong = stiffness / weights[:, None]
    ratio = np.diag(strong)
    laplace = (
        np.kron(np.kron(strong, identity), identity)
        + np.kron(np.kron(identity, strong), identity)
        + np.kron(np.kron(identity, identity), strong)
    )
    diagonal = (
        LAMBDA_H + ratio[:, None, None] + ratio[None, :, None] + ratio[None, None, :]
    ).reshape(512)
    share = np.ones((8, 64))
    share[0] = 0.5
    share[7] = 0.5
    smooth = -DAMPING_RATIO * (share.reshape(512) / diagonal)[:, None] * laplace
    quad = smooth.reshape(8, 64, 8, 64)
    near = quad[:4, :, :4, :]
    far = quad[:4, :, 7:3:-1, :]
    even = (0.5 * (near + far)).reshape(256, 256)
    odd = (0.5 * (near - far)).reshape(256, 256)
    carry = -CARRY_STEP_SIZE * gradient
    from_even = 0.5 * (carry[:4, :4] + carry[:4, 7:3:-1])
    from_odd = 0.5 * (carry[:4, :4] - carry[:4, 7:3:-1])
    weight_matrix = np.diag(weights)
    in_plane = (np.kron(stiffness, weight_matrix) + np.kron(weight_matrix, stiffness)) / np.kron(
        weights, weights
    )[:, None]
    through = np.array([[-1.0, 1.0], [1.0, -1.0]])
    plate_op = -np.kron(np.eye(2), in_plane) + COUPLE * np.kron(through, np.eye(64))
    even_parts = split_pair(even)
    odd_parts = split_pair(odd)
    smoothing = np.stack(
        [np.concatenate(even_parts, 1), np.concatenate(odd_parts, 1)]
    )
    plate_parts = np.concatenate(split_pair(plate_op), 1)
    return from_even, from_odd, smoothing, plate_parts


def halves(value):
    high = value.astype(jnp.bfloat16)
    low = (value - high.astype(jnp.float32)).astype(jnp.bfloat16)
    return high, low


def dot32(a, b):
    return jnp.dot(a, b, preferred_element_type=jnp.float32)


def edge_kernel(t_low, t_high, v_low, v_high, to_next, to_prev):
    tl = t_low[...].T
    vl = v_low[...].T
    th = t_high[...].T
    vh = v_high[...].T
    to_prev[0:2, :] = tl[0:2, :]
    to_prev[2:4, :] = vl[0:2, :]
    to_prev[4:8, :] = jnp.zeros((4, 512), jnp.float32)
    to_next[0:2, :] = th[126:128, :]
    to_next[2:4, :] = vh[126:128, :]
    to_next[4:8, :] = jnp.zeros((4, 512), jnp.float32)


def rank_kernel(owner, position):
    wide = 256
    row = lax.broadcasted_iota(jnp.int32, (wide, wide), 0)
    col = lax.broadcasted_iota(jnp.int32, (wide, wide), 1)
    upto = (row <= col).astype(jnp.float32).astype(jnp.bfloat16)
    name = lax.broadcasted_iota(jnp.int32, (128, LANES), 0)
    before = jnp.zeros((128, 1), jnp.float32)
    for step in range(8):
        pair = [
            (name == owner[2 * step + i : 2 * step + i + 1, :]).astype(jnp.float32)
            for i in range(2)
        ]
        hot = jnp.concatenate(pair, axis=1)
        seen = dot32(hot.astype(jnp.bfloat16), upto)
        rank = jnp.sum(hot * (seen + before), axis=0, keepdims=True) - 1.0
        before = before + seen[:, wide - 1 : wide]
        for i in range(2):
            at = slice(2 * step + i, 2 * step + i + 1)
            position[at, :] = owner[at, :] * 32 + rank[:, i * LANES : (i + 1) * LANES].astype(
                jnp.int32
            )


def sweep_kernel(
    from_even,
    from_odd,
    ends,
    t_in,
    v_in,
    film,
    from_prev,
    from_next,
    smoothing,
    position,
    t_out,
    wall_out,
    sending,
    tx,
    vx,
    adv,
    high,
    low,
    even,
    odd,
    edge,
    faces,
    sems,
    out_sems,
):
    count = t_in.shape[-1]
    blocks = count // LANES + 1
    loads = []
    for b in range(8):
        pair = (
            pltpu.make_async_copy(t_in.at[:, b], tx.at[:, b, :, pl.ds(0, count)], sems.at[0, b]),
            pltpu.make_async_copy(v_in.at[:, b], vx.at[:, b, :, pl.ds(0, count)], sems.at[1, b]),
        )
        for copy in pair:
            copy.start()
        loads.append(pair)
    edge[...] = jnp.zeros_like(edge)
    edge[0:2, :] = from_next[0:2, :]
    edge[126:128, :] = from_prev[0:2, :]
    tx[:, :, :, pl.ds(count, LANES)] = edge[...].T.reshape(8, 8, 8, LANES)
    edge[0:2, :] = from_next[2:4, :]
    edge[126:128, :] = from_prev[2:4, :]
    vx[:, :, :, pl.ds(count, LANES)] = edge[...].T.reshape(8, 8, 8, LANES)
    sending[...] = jnp.zeros_like(sending)
    lane = lax.broadcasted_iota(jnp.int32, (8, LANES), 1)
    is_first = ends[0] == 1
    is_last = ends[1] == 1

    def carry(pair, lanes):
        at = pl.ds(2 * pair, 2)
        t = [tx[a, at, :, lanes].reshape(16, LANES) for a in range(8)]
        v = [vx[a, at, :, lanes].reshape(16, LANES) for a in range(8)]
        e = [t[k] + t[7 - k] for k in range(4)]
        o = [t[k] - t[7 - k] for k in range(4)]
        for i in range(4):
            p = sum(float(from_even[i, j]) * e[j] for j in range(4))
            q = sum(float(from_odd[i, j]) * o[j] for j in range(4))
            near = t[i] + v[i] * (q + p)
            far = t[7 - i] + v[7 - i] * (q - p)
            adv[i, at, :, lanes] = near.reshape(2, 8, LANES)
            adv[7 - i, at, :, lanes] = far.reshape(2, 8, LANES)
            for number, part in enumerate((near + far, near - far)):
                first, second = halves(part)
                rows = pl.ds(256 * number + 64 * i + 16 * pair, 16)
                high[rows, lanes] = first
                low[rows, lanes] = second

    for sweep in range(SWEEPS):
        for pair in range(4):
            if sweep == 0:
                for b in (2 * pair, 2 * pair + 1):
                    for copy in loads[b]:
                        copy.wait()
            for block in range(blocks):
                carry(pair, pl.ds(block * LANES, LANES))
        for number, target in enumerate((even, odd)):
            rows = pl.ds(256 * number, 256)
            first = smoothing[number, :, pl.ds(0, 256)]
            second = smoothing[number, :, pl.ds(256, 256)]
            target[...] = (
                dot32(first, high[rows, :]) + dot32(second, high[rows, :]) + dot32(first, low[rows, :])
            )
        for b in range(8):
            bottom, top, bottom_moved, top_moved = [], [], [], []
            for block in range(blocks):
                lanes = pl.ds(block * LANES, LANES)
                e = even[pl.ds(8 * b, 8), lanes]
                o = odd[pl.ds(8 * b, 8), lanes]
                bottom.append(e + o)
                top.append(e - o)
                bottom_moved.append(pltpu.roll(bottom[-1], LANES - 1, 1))
                top_moved.append(pltpu.roll(top[-1], 1, 1))
            for block in range(blocks):
                lanes = pl.ds(block * LANES, LANES)
                before = jnp.where(lane == 0, top_moved[block - 1], top_moved[block])
                after = jnp.where(
                    lane == LANES - 1, bottom_moved[(block + 1) % blocks], bottom_moved[block]
                )
                if block == 0:
                    before = jnp.where((lane == 0) & is_first, bottom[0], before)
                if block == blocks - 2:
                    after = jnp.where((lane == LANES - 1) & is_last, top[block], after)
                tx[0, b, :, lanes] = adv[0, b, :, lanes] + (bottom[block] + before)
                tx[7, b, :, lanes] = adv[7, b, :, lanes] + (top[block] + after)
                for k in range(1, 4):
                    e = even[pl.ds(64 * k + 8 * b, 8), lanes]
                    o = odd[pl.ds(64 * k + 8 * b, 8), lanes]
                    tx[k, b, :, lanes] = adv[k, b, :, lanes] + (e + o)
                    tx[7 - k, b, :, lanes] = adv[7 - k, b, :, lanes] + (e - o)

    stores = [
        pltpu.make_async_copy(tx.at[:, b, :, pl.ds(0, count)], t_out.at[:, b], out_sems.at[b])
        for b in range(8)
    ]
    for copy in stores:
        copy.start()
    for block in range(blocks - 1):
        lanes = pl.ds(block * LANES, LANES)
        for side in range(2):
            wall = tx[:, 7 * side, :, lanes].reshape(64, LANES)
            wall_out[pl.ds(64 * side, 64), lanes] = wall
            layer = film[pl.ds(64 * side, 64), lanes]
            faces[side, lanes, :] = jnp.concatenate([layer, layer * wall], axis=0).T

    def scatter(i, _):
        for j in range(128):
            spot = position[i, j]
            sending[pl.ds(spot, 1), :] = faces[j % 2, pl.ds(i * 64 + j // 2, 1), :]
        return 0

    lax.fori_loop(0, 16, scatter, 0)
    for copy in stores:
        copy.wait()


def owner_kernel(arrived, cell, plate, conductivity, plate_op, sheet, returning, hot, parts):
    name = lax.broadcasted_iota(jnp.int32, (512, LANES), 0)
    for i in range(32):
        hot[:, pl.ds(i * LANES, LANES)] = (
            (name == cell[i : i + 1, :]).astype(jnp.float32).astype(jnp.bfloat16)
        )
    for half in range(2):
        for i in range(16):
            block = arrived[pl.ds(8 * i, 8), pl.ds(16 * half, 16), :].reshape(128, LANES)
            first, second = halves(block)
            rows = pl.ds((16 * half + i) * 128, 128)
            parts[rows, pl.ds(0, LANES)] = first
            parts[rows, pl.ds(LANES, LANES)] = second
    both = dot32(hot[...], parts[...])
    total = (both[:, :LANES] + both[:, LANES:]).T
    film_sum = total[:64]
    heat_sum = total[64:]
    contact = (plate[0:64, :] + CONTACT * heat_sum) / (1.0 + CONTACT * film_sum)
    relaxed = jnp.concatenate([contact, plate[64:128, :]], axis=0)
    first, second = halves(relaxed)
    op_first = plate_op[:, pl.ds(0, 128)]
    op_second = plate_op[:, pl.ds(128, 128)]
    spread = dot32(op_first, first) + dot32(op_second, first) + dot32(op_first, second)
    conducted = relaxed + DT_PLATE * conductivity[...] * spread
    sheet[...] = conducted
    first, second = halves(conducted[:64])
    both = dot32(jnp.concatenate([first, second], axis=0), hot[...])
    seen = both[:64] + both[64:]
    for i in range(16):
        block = jnp.concatenate(
            [seen[:, i * 128 : (i + 1) * 128], seen[:, 2048 + i * 128 : 2048 + (i + 1) * 128]], axis=0
        )
        returning[pl.ds(i * 128, 128), :] = block.T


def finish_kernel(returned, position, film, wall, t_in, t_out, contact_out, rows, gathered, out, sems):
    del t_in
    lane = lax.broadcasted_iota(jnp.int32, (16, LANES), 1)
    for q in range(128):
        block = returned[pl.ds(16 * q, 16), :]
        turned = pltpu.roll(block, 64, 1)
        rows[pl.ds(32 * q, 16), :] = jnp.where(lane < 64, block, turned)
        rows[pl.ds(32 * q + 16, 16), :] = jnp.where(lane < 64, turned, block)
    one = lax.broadcasted_iota(jnp.int32, (1, LANES), 1)

    def gather(i, _):
        for j in range(64):
            low = rows[pl.ds(position[i, 2 * j], 1), :]
            high = rows[pl.ds(position[i, 2 * j + 1], 1), :]
            gathered[pl.ds(i * 64 + j, 1), :] = jnp.where(one < 64, low, high)
        return 0

    lax.fori_loop(0, 16, gather, 0)
    for block in range(8):
        lanes = pl.ds(block * LANES, LANES)
        contact = gathered[lanes, :].T
        contact_out[:, lanes] = contact
        own = wall[:, lanes]
        out[:, lanes] = own + MIXING_WEIGHT * (film[:, lanes] * (contact - own))
    copies = []
    for side in range(2):
        for a in range(8):
            copies.append(
                pltpu.make_async_copy(
                    out.at[pl.ds(64 * side + 8 * a, 8)], t_out.at[a, 7 * side], sems.at[side, a]
                )
            )
    for copy in copies:
        copy.start()
    for copy in copies:
        copy.wait()


def vmem():
    return pl.BlockSpec(memory_space=pltpu.VMEM)


def smem():
    return pl.BlockSpec(memory_space=pltpu.SMEM)


def anywhere():
    return pl.BlockSpec(memory_space=pl.ANY)


def params():
    return pltpu.CompilerParams(vmem_limit_bytes=VMEM_LIMIT)


def shards(warmth, velocity, wall_film, face_owner, plate_temp, conductivity, plate_cell):
    from_even, from_odd, smoothing, plate_op = gll_tables()
    f32 = jnp.float32
    count = warmth.shape[1]
    axes = ("flow", "grp")
    devices = lax.axis_size(axes)
    me = lax.axis_index(axes)
    last = count // LANES - 1
    side = jax.ShapeDtypeStruct((8, 512), f32)
    to_next, to_prev = pl.pallas_call(
        edge_kernel,
        grid=(1,),
        out_shape=(side, side),
        in_specs=[
            pl.BlockSpec((512, LANES), lambda i: (0, 0)),
            pl.BlockSpec((512, LANES), lambda i: (0, last)),
            pl.BlockSpec((512, LANES), lambda i: (0, 0)),
            pl.BlockSpec((512, LANES), lambda i: (0, last)),
        ],
        out_specs=[pl.BlockSpec((8, 512), lambda i: (0, 0))] * 2,
        compiler_params=params(),
        name="edges",
    )(warmth, warmth, velocity, velocity)
    up = [(i, i + 1) for i in range(devices - 1)]
    down = [(j, i) for i, j in up]
    from_prev = lax.ppermute(to_next, axes, up)
    from_next = lax.ppermute(to_prev, axes, down)
    position = pl.pallas_call(
        rank_kernel,
        out_shape=jax.ShapeDtypeStruct((16, 128), jnp.int32),
        in_specs=[vmem()],
        out_specs=vmem(),
        compiler_params=params(),
        name="ranks",
    )(face_owner.reshape(16, 128))
    ends = jnp.stack([me == 0, me == devices - 1]).astype(jnp.int32)
    wide = count + LANES
    t_new, wall, sending = pl.pallas_call(
        functools.partial(sweep_kernel, from_even, from_odd),
        out_shape=(
            jax.ShapeDtypeStruct((8, 8, 8, count), f32),
            jax.ShapeDtypeStruct((128, count), f32),
            jax.ShapeDtypeStruct((4096, LANES), f32),
        ),
        in_specs=[smem(), anywhere(), anywhere(), vmem(), vmem(), vmem(), vmem(), smem()],
        out_specs=(anywhere(), vmem(), vmem()),
        scratch_shapes=[
            pltpu.VMEM((8, 8, 8, wide), f32),
            pltpu.VMEM((8, 8, 8, wide), f32),
            pltpu.VMEM((8, 8, 8, wide), f32),
            pltpu.VMEM((512, wide), jnp.bfloat16),
            pltpu.VMEM((512, wide), jnp.bfloat16),
            pltpu.VMEM((256, wide), f32),
            pltpu.VMEM((256, wide), f32),
            pltpu.VMEM((128, 512), f32),
            pltpu.VMEM((2, count, LANES), f32),
            pltpu.SemaphoreType.DMA((2, 8)),
            pltpu.SemaphoreType.DMA((8,)),
        ],
        compiler_params=params(),
        name="sweeps",
    )(
        ends,
        warmth.reshape(8, 8, 8, count),
        velocity.reshape(8, 8, 8, count),
        wall_film,
        from_prev,
        from_next,
        jnp.asarray(smoothing),
        position,
    )
    arrived = lax.all_to_all(
        sending.reshape(128, 32, LANES), axes, split_axis=0, concat_axis=0, tiled=True
    )
    cell = plate_cell.reshape(128, 2, 16).transpose(1, 0, 2).reshape(32, LANES)
    sheet, returning = pl.pallas_call(
        owner_kernel,
        out_shape=(
            jax.ShapeDtypeStruct((128, 512), f32),
            jax.ShapeDtypeStruct((2048, LANES), f32),
        ),
        in_specs=[vmem()] * 5,
        out_specs=(vmem(), vmem()),
        scratch_shapes=[
            pltpu.VMEM((512, 4096), jnp.bfloat16),
            pltpu.VMEM((4096, 256), jnp.bfloat16),
        ],
        compiler_params=params(),
        name="plates",
    )(arrived, cell, plate_temp, conductivity, jnp.asarray(plate_op))
    returned = lax.all_to_all(
        returning.reshape(128, 16, LANES), axes, split_axis=0, concat_axis=0, tiled=True
    )
    coolant, boundary = pl.pallas_call(
        finish_kernel,
        out_shape=(
            jax.ShapeDtypeStruct((8, 8, 8, count), f32),
            jax.ShapeDtypeStruct((128, count), f32),
        ),
        in_specs=[vmem(), smem(), vmem(), vmem(), anywhere()],
        out_specs=(anywhere(), vmem()),
        scratch_shapes=[
            pltpu.VMEM((4096, LANES), f32),
            pltpu.VMEM((count, LANES), f32),
            pltpu.VMEM((128, count), f32),
            pltpu.SemaphoreType.DMA((2, 8)),
        ],
        input_output_aliases={4: 0},
        compiler_params=params(),
        name="finish",
    )(returned.reshape(2048, LANES), position, wall_film, wall, t_new)
    return coolant.reshape(512, count), boundary, sheet


def solution(mesh):
    placed = (
        P(None, ("flow", "grp")),
        P(None, ("flow", "grp")),
        P(None, ("flow", "grp")),
        P(("flow", "grp"), None),
        P(None, ("flow", "grp")),
        P(None, ("flow", "grp")),
        P(("flow", "grp")),
    )
    return jax.shard_map(
        shards,
        mesh=mesh,
        in_specs=placed,
        out_specs=(P(None, ("flow", "grp")), P(None, ("flow", "grp")), P(None, ("flow", "grp"))),
        check_vma=False,
    )
```

profile of v0, /device:TPU:1, one launch (start us, length us, event | category | flops | bytes accessed | tf_op | source)
XLA Modules:
  0.0 105.5 jit_solution(1206068390700129790)
XLA Ops:
  0.6 2.2 %edges.1 = (f32[8,512]{1,0:T(8,128)}, f32[8,512]{1,0:T(8,128)}) custom-call(f32[512,1024]{1,0:T(8,128)} %t_high.1, f32[512,1024]{1,0:T(8,128)} %t_high.1, f32[512,1024]{1,0:T(8,128)} %v_high.1, f32[512,1024]{1,0:T(8,128)} %v_high.1), custom_call_target="tpu_custom_call" | custom-call | tf_op jit(solution)/shard_map/edges/pallas_call | solution.py:377
  2.8 3.9 %collective-permute-start = (f32[8,512]{1,0:T(8,128)}, f32[8,512]{1,0:T(8,128)S(1)}, u32[]{:S(2)}, u32[]{:S(2)}) collective-permute-start(f32[8,512]{1,0:T(8,128)} %get-tuple-element.12), channel_id=1, source_target_pairs={{0,1},{1,2},{2,3},{3,4},{4,5},{5,6},{6,7},{7,8},{8,9},{9,10},{10,1... | collective-permute-start | bytes 49160 | tf_op jit(solution)/shard_map/ppermute | solution.py:393
  6.7 3.7 %collective-permute-start.1 = (f32[8,512]{1,0:T(8,128)}, f32[8,512]{1,0:T(8,128)S(1)}, u32[]{:S(2)}, u32[]{:S(2)}) collective-permute-start(f32[8,512]{1,0:T(8,128)} %get-tuple-element.13), channel_id=1, source_target_pairs={{1,0},{2,1},{3,2},{4,3},{5,4},{6,5},{7,6},{8,7},{9,8},{10,9},{11,1... | collective-permute-start | bytes 49160 | tf_op jit(solution)/shard_map/ppermute | solution.py:394
  10.5 0.7 add_convert_fusion.ends
  11.1 1.7 %ranks.1.position = s32[16,128]{1,0:T(8,128)} custom-call(s32[16,128]{1,0:T(8,128)} %bitcast.17), custom_call_target="tpu_custom_call" | custom-call | tf_op jit(solution)/shard_map/ranks/pallas_call | solution.py:395
  12.9 0.0 collective-permute-done.from_prev
  12.9 0.0 copy-start.1
  12.9 0.0 collective-permute-done.1.from_next
  12.9 0.0 copy-start.2
  12.9 0.6 copy-done.1
  13.5 0.0 copy-done.2
  13.5 11.0 %sweeps.1 = (f32[8,8,8,1024]{3,2,1,0:T(8,128)}, f32[128,1024]{1,0:T(8,128)}, f32[4096,128]{1,0:T(8,128)}) custom-call(s32[2]{0:T(128)} %add_convert_fusion.ends, f32[8,8,8,1024]{3,2,1,0:T(8,128)} %bitcast.10, f32[8,8,8,1024]{3,2,1,0:T(8,128)} %bitcast.11, f32[128,1024]{1,0:T(8,128)} %film.3, f32[8,512]{1,0:T(8,128)} %copy-done.1, f32[8,512]{1,0:T(8,128)} %copy-done.2, ...), custom_call_target="tpu_custom_call" | custom-call | tf_op jit(solution)/shard_map/sweeps/pallas_call | solution.py:405
  24.5 0.0 copy-start.3
  24.6 12.1 %all-to-all-start = ((f32[128,32,128]{2,1,0:T(8,128)}), f32[128,32,128]{2,1,0:T(8,128)S(1)}, u32[]{:S(2)}, u32[]{:S(2)}) async-start(f32[128,32,128]{2,1,0:T(8,128)} %bitcast.14), calls=%async_computation | async-start | bytes 4194304 | tf_op jit(solution)/shard_map/all_to_all | solution.py:439
  36.6 0.0 copy-done.3
  36.7 0.2 reshape.37
  36.9 0.7 reshape.38.cell
  37.6 30.0 %all-to-all-done.arrived = f32[128,32,128]{2,1,0:T(8,128)S(1)} async-done(((f32[128,32,128]{2,1,0:T(8,128)}), f32[128,32,128]{2,1,0:T(8,128)S(1)}, u32[]{:S(2)}, u32[]{:S(2)}) %all-to-all-start) | async-done | bytes 2097184 | tf_op jit(solution)/shard_map/all_to_all | solution.py:439
  67.6 0.0 copy-start
  67.6 1.3 %copy-done = f32[128,32,128]{2,1,0:T(8,128)} copy-done((f32[128,32,128]{2,1,0:T(8,128)}, f32[128,32,128]{2,1,0:T(8,128)S(1)}, u32[]{:S(2)}) %copy-start) | copy-done | bytes 2097176
  69.0 6.6 %plates.1 = (f32[128,512]{1,0:T(8,128)}, f32[2048,128]{1,0:T(8,128)}) custom-call(f32[128,32,128]{2,1,0:T(8,128)} %copy-done, s32[32,128]{1,0:T(8,128)} %reshape.38.cell, f32[128,512]{1,0:T(8,128)} %plate.1, f32[128,512]{1,0:T(8,128)} %conductivity.1, bf16[128,256]{1,0:T(8,128)(2,1)} %constant.20.clone.plate_op), custom_call_target="tpu_custom_call" | custom-call | tf_op jit(solution)/shard_map/plates/pallas_call | solution.py:443
  75.6 24.5 %all_to_all.10 = f32[128,16,128]{2,1,0:T(8,128)} all-to-all(f32[128,16,128]{2,1,0:T(8,128)} %bitcast.15), channel_id=1, replica_groups=mesh['flow'=32,'grp'=4] {'flow','grp'}, dimensions={0} | all-to-all | bytes 2097152 | tf_op jit(solution)/shard_map/all_to_all | solution.py:458
  100.1 5.5 %finish.1 = (f32[8,8,8,1024]{3,2,1,0:T(8,128)}, f32[128,1024]{1,0:T(8,128)}) custom-call(f32[2048,128]{1,0:T(8,128)} %bitcast.12, s32[16,128]{1,0:T(8,128)} %ranks.1.position, f32[128,1024]{1,0:T(8,128)} %film.3, f32[128,1024]{1,0:T(8,128)} %get-tuple-element.16.wall, f32[8,8,8,1024]{3,2,1,0:T(8,128)} %get-tuple-element.17.t_in), custom_call_target="tpu_custom_call", output_to_operand_aliasing={{0}: (4, {})} | custom-call | tf_op jit(solution)/shard_map/finish/pallas_call | solution.py:461
  (1 shorter events, 0.0 us)
Async XLA Ops:
  2.8 10.1 %collective-permute-start = (f32[8,512]{1,0:T(8,128)}, f32[8,512]{1,0:T(8,128)S(1)}, u32[]{:S(2)}, u32[]{:S(2)}) collective-permute-start(f32[8,512]{1,0:T(8,128)} %get-tuple-element.12), channel_id=1, source_target_pairs={{0,1},{1,2},{2,3},{3,4},{4,5},{5,6},{6,7},{7,8},{8,9},{9,10},{10,1... | collective-permute-start | bytes 49160 | tf_op jit(solution)/shard_map/ppermute | solution.py:393
  6.7 6.1 %collective-permute-start.1 = (f32[8,512]{1,0:T(8,128)}, f32[8,512]{1,0:T(8,128)S(1)}, u32[]{:S(2)}, u32[]{:S(2)}) collective-permute-start(f32[8,512]{1,0:T(8,128)} %get-tuple-element.13), channel_id=1, source_target_pairs={{1,0},{2,1},{3,2},{4,3},{5,4},{6,5},{7,6},{8,7},{9,8},{10,9},{11,1... | collective-permute-start | bytes 49160 | tf_op jit(solution)/shard_map/ppermute | solution.py:394
  12.9 0.6 copy-start.1
  12.9 0.6 copy-start.2
  24.5 12.1 %copy-start.3 = (s32[4096]{0:T(1024)S(1)}, s32[4096]{0:T(1024)}, u32[]{:S(2)}) copy-start(s32[4096]{0:T(1024)} %param.15) | copy-start | bytes 49156
  24.6 43.1 %all-to-all-start = ((f32[128,32,128]{2,1,0:T(8,128)}), f32[128,32,128]{2,1,0:T(8,128)S(1)}, u32[]{:S(2)}, u32[]{:S(2)}) async-start(f32[128,32,128]{2,1,0:T(8,128)} %bitcast.14), calls=%async_computation | async-start | bytes 4194304 | tf_op jit(solution)/shard_map/all_to_all | solution.py:439
  67.6 1.3 %copy-start = (f32[128,32,128]{2,1,0:T(8,128)}, f32[128,32,128]{2,1,0:T(8,128)S(1)}, u32[]{:S(2)}) copy-start(f32[128,32,128]{2,1,0:T(8,128)S(1)} %all-to-all-done.arrived) | copy-start | bytes 6291460
where the time goes:
time: 106 us
  waiting for transfers between devices  30 us (28%)
  Pallas kernels  27 us (25%)
  blocking collectives  24.5 us (23%)
  starting transfers between devices  19.8 us (19%)
  local copies, waits for them, and re-layouts  2.86 us (3%)
    all_to_all x1, waiting for transfers between devices, shards(): lax.all_to_all(sending.reshape(128, 32, LANES), axes, split_axis=0, conca...  30 us
    all_to_all x1, blocking collectives, shards(): lax.all_to_all(returning.reshape(128, 16, LANES), axes, split_axis=0, con...  24.5 us
    all_to_all x1, starting transfers between devices, shards(): lax.all_to_all(sending.reshape(128, 32, LANES), axes, split_axis=0, conca...  12.1 us
    pallas_call x1, Pallas kernels, shards(): pl.pallas_call(functools.partial(sweep_kernel, from_even, from_odd), out_...  11 us
    pallas_call x1, Pallas kernels, shards(): pl.pallas_call(owner_kernel, out_shape=(jax.ShapeDtypeStruct((128, 512),...  6.63 us
    pallas_call x1, Pallas kernels, shards(): pl.pallas_call(finish_kernel, out_shape=(jax.ShapeDtypeStruct((8, 8, 8, c...  5.47 us
    ppermute x1, starting transfers between devices, shards(): from_prev = lax.ppermute(to_next, axes, up)  3.94 us
    ppermute x1, starting transfers between devices, shards(): from_next = lax.ppermute(to_prev, axes, down)  3.75 us
  transfers between devices with their start and end apart: 3, of which 1 were waited for; matrix products, arithmetic and copies ran while one was open for 1% of the time, Pallas kernels for 2%

commit v1 on v0

v1 whole, which is shorter than its diff:
```python
import functools

import jax
import jax.numpy as jnp
import ml_dtypes
import numpy as np
from jax import lax
from jax.experimental import pallas as pl
from jax.experimental.pallas import tpu as pltpu
from jax.sharding import PartitionSpec as P

SWEEPS = 2
LAMBDA_H = 4.0
DAMPING_RATIO = 0.5
CARRY_STEP_SIZE = 0.05
CONTACT = 0.1
DT_PLATE = 0.0008
COUPLE = 20.0
MIXING_WEIGHT = 0.5
GLL_POINTS = (
    -1.0,
    -0.8717401485096066,
    -0.5917001814331423,
    -0.2092992179024789,
    0.2092992179024789,
    0.5917001814331423,
    0.8717401485096066,
    1.0,
)
GLL_WEIGHTS = (
    0.03571428571428571,
    0.2107042271435061,
    0.3411226924835044,
    0.4124587946587038,
    0.4124587946587038,
    0.3411226924835044,
    0.2107042271435061,
    0.03571428571428571,
)
LANES = 128


def split_pair(table):
    high = np.asarray(table, np.float32).astype(ml_dtypes.bfloat16)
    low = (np.asarray(table, np.float64) - high.astype(np.float64)).astype(np.float32)
    return high, low.astype(ml_dtypes.bfloat16)


def gll_tables():
    points = np.array(GLL_POINTS)
    weights = np.array(GLL_WEIGHTS)
    identity = np.eye(8)
    spread = points[:, None] - points[None, :] + identity
    bary_weight = 1.0 / np.prod(spread, axis=1)
    gradient = bary_weight[None, :] / bary_weight[:, None] / spread
    gradient = gradient * (1.0 - identity)
    gradient = gradient - identity * gradient.sum(axis=1)[:, None]
    stiffness = gradient.T * weights[None, :] @ gradient
    strong = stiffness / weights[:, None]
    ratio = np.diag(strong)
    laplace = (
        np.kron(np.kron(strong, identity), identity)
        + np.kron(np.kron(identity, strong), identity)
        + np.kron(np.kron(identity, identity), strong)
    )
    diagonal = (
        LAMBDA_H + ratio[:, None, None] + ratio[None, :, None] + ratio[None, None, :]
    ).reshape(512)
    share = np.ones((8, 64))
    share[0] = 0.5
    share[7] = 0.5
    smooth = -DAMPING_RATIO * (share.reshape(512) / diagonal)[:, None] * laplace
    quad = smooth.reshape(8, 64, 8, 64)
    near = quad[:4, :, :4, :]
    far = quad[:4, :, 7:3:-1, :]
    even = (0.5 * (near + far)).reshape(256, 256)
    odd = (0.5 * (near - far)).reshape(256, 256)
    carry = -CARRY_STEP_SIZE * gradient
    from_even = 0.5 * (carry[:4, :4] + carry[:4, 7:3:-1])
    from_odd = 0.5 * (carry[:4, :4] - carry[:4, 7:3:-1])
    weight_matrix = np.diag(weights)
    in_plane = (np.kron(stiffness, weight_matrix) + np.kron(weight_matrix, stiffness)) / np.kron(
        weights, weights
    )[:, None]
    through = np.array([[-1.0, 1.0], [1.0, -1.0]])
    plate_op = -np.kron(np.eye(2), in_plane) + COUPLE * np.kron(through, np.eye(64))
    even_parts = split_pair(even)
    odd_parts = split_pair(odd)
    smoothing = np.stack(
        [np.concatenate(even_parts, 1), np.concatenate(odd_parts, 1)]
    )
    plate_parts = np.concatenate(split_pair(plate_op), 1)
    return from_even, from_odd, smoothing, plate_parts


def halves(value):
    high = value.astype(jnp.bfloat16)
    low = (value - high.astype(jnp.float32)).astype(jnp.bfloat16)
    return high, low


def dot32(a, b):
    return jnp.dot(a, b, preferred_element_type=jnp.float32)


def edge_kernel(t_in, v_in, to_next, to_prev, held, sems):
    count = t_in.shape[1]
    copies = []
    for i, array in enumerate((t_in, v_in)):
        for j, start in enumerate((0, count - LANES)):
            copy = pltpu.make_async_copy(
                array.at[:, pl.ds(start, LANES)], held.at[i, j], sems.at[i, j]
            )
            copy.start()
            copies.append(copy)
    for copy in copies:
        copy.wait()
    for i in range(2):
        to_prev[pl.ds(2 * i, 2), :] = held[i, 0].T[0:2, :]
        to_next[pl.ds(2 * i, 2), :] = held[i, 1].T[126:128, :]
    to_prev[4:8, :] = jnp.ones((4, 512), jnp.float32)
    to_next[4:8, :] = jnp.ones((4, 512), jnp.float32)


def fill_positions(owner, position):
    wide = 256
    row = lax.broadcasted_iota(jnp.int32, (wide, wide), 0)
    col = lax.broadcasted_iota(jnp.int32, (wide, wide), 1)
    upto = (row <= col).astype(jnp.float32).astype(jnp.bfloat16)
    name = lax.broadcasted_iota(jnp.int32, (128, LANES), 0)
    before = jnp.zeros((128, 1), jnp.float32)
    for step in range(8):
        pair = [
            (name == owner[2 * step + i : 2 * step + i + 1, :]).astype(jnp.float32)
            for i in range(2)
        ]
        hot = jnp.concatenate(pair, axis=1)
        seen = dot32(hot.astype(jnp.bfloat16), upto)
        rank = jnp.sum(hot * (seen + before), axis=0, keepdims=True) - 1.0
        before = before + seen[:, wide - 1 : wide]
        for i in range(2):
            at = slice(2 * step + i, 2 * step + i + 1)
            position[at, :] = owner[at, :] * 32 + rank[:, i * LANES : (i + 1) * LANES].astype(
                jnp.int32
            )


def carry(from_even, from_odd, t, v, adv, high, low, pair, block):
    at = pl.ds(2 * pair, 2)
    lanes = pl.ds(block * LANES, LANES)
    e = [t[k] + t[7 - k] for k in range(4)]
    o = [t[k] - t[7 - k] for k in range(4)]
    for i in range(4):
        p = sum(float(from_even[i, j]) * e[j] for j in range(4))
        q = sum(float(from_odd[i, j]) * o[j] for j in range(4))
        near = t[i] + v[i] * (q + p)
        far = t[7 - i] + v[7 - i] * (q - p)
        adv[i, at, :, lanes] = near.reshape(2, 8, LANES)
        adv[7 - i, at, :, lanes] = far.reshape(2, 8, LANES)
        for number, part in enumerate((near + far, near - far)):
            first, second = halves(part)
            rows = pl.ds(256 * number + 64 * i + 16 * pair, 16)
            high[rows, lanes] = first
            low[rows, lanes] = second


def smooth(smoothing, high, low, even, odd, group):
    lanes = pl.ds(group[0] * LANES, len(group) * LANES)
    for number, target in enumerate((even, odd)):
        rows = pl.ds(256 * number, 256)
        first = smoothing[number, :, pl.ds(0, 256)]
        second = smoothing[number, :, pl.ds(256, 256)]
        target[:, lanes] = (
            dot32(first, high[rows, lanes])
            + dot32(second, high[rows, lanes])
            + dot32(first, low[rows, lanes])
        )


def slab(array, a, pair, block):
    return array[a, pl.ds(2 * pair, 2), :, pl.ds(block * LANES, LANES)].reshape(16, LANES)


def begin_kernel(
    from_even,
    from_odd,
    t_in,
    v_in,
    film_in,
    smoothing_in,
    owner,
    v,
    adv,
    even,
    odd,
    film,
    smoothing,
    position,
    t,
    high,
    low,
    sems,
):
    count = t_in.shape[-1]
    groups = [[2 * i, 2 * i + 1] for i in range(count // LANES // 2)]
    loads = []
    for number, group in enumerate(groups):
        lanes = pl.ds(group[0] * LANES, 2 * LANES)
        loads.append(
            (
                pltpu.make_async_copy(t_in.at[:, :, :, lanes], t.at[:, :, :, lanes], sems.at[0, number]),
                pltpu.make_async_copy(v_in.at[:, :, :, lanes], v.at[:, :, :, lanes], sems.at[1, number]),
            )
        )
    smoothing_copy = pltpu.make_async_copy(smoothing_in, smoothing, sems.at[0, 4])
    film_copy = pltpu.make_async_copy(film_in, film, sems.at[1, 4])
    for copy in loads[0] + (smoothing_copy,) + sum(loads[1:], ()) + (film_copy,):
        copy.start()
    fill_positions(owner, position)
    for number, group in enumerate(groups):
        for copy in loads[number]:
            copy.wait()
        for pair in range(4):
            for block in group:
                carry(
                    from_even,
                    from_odd,
                    [slab(t, a, pair, block) for a in range(8)],
                    [slab(v, a, pair, block) for a in range(8)],
                    adv,
                    high,
                    low,
                    pair,
                    block,
                )
        if number == 0:
            smoothing_copy.wait()
        smooth(smoothing, high, low, even, odd, group)
    film_copy.wait()


def sweep_kernel(
    from_even,
    from_odd,
    v,
    adv,
    even_first,
    odd_first,
    film,
    smoothing,
    from_prev,
    from_next,
    position_in,
    t_out,
    wall_out,
    sending,
    position,
    wall,
    t_edge,
    v_edge,
    adv_edge,
    high_edge,
    low_edge,
    even_edge,
    odd_edge,
    t_new,
    adv_second,
    high,
    low,
    even_second,
    odd_second,
    edge,
    faces,
    in_sem,
    out_sems,
):
    position_copy = pltpu.make_async_copy(position_in, position, in_sem)
    position_copy.start()
    count = v.shape[-1]
    inner = count // LANES
    blocks = inner + 1
    groups = [[2 * i, 2 * i + 1] for i in range(inner // 2)]
    edge[...] = jnp.zeros_like(edge)
    for i, array in enumerate((t_edge, v_edge)):
        edge[0:2, :] = from_next[pl.ds(2 * i, 2), :]
        edge[126:128, :] = from_prev[pl.ds(2 * i, 2), :]
        array[...] = edge[...].T.reshape(8, 8, 8, LANES)
    sending[...] = jnp.zeros_like(sending)
    lane = lax.broadcasted_iota(jnp.int32, (16, LANES), 1)
    is_first = (lane == 0) & (from_prev[4:5, 0:LANES] == 0.0)
    is_last = (lane == LANES - 1) & (from_next[4:5, 0:LANES] == 0.0)

    def part(even, odd, k, pair, block):
        at = (pl.ds(64 * k + 16 * pair, 16), pl.ds((block % inner) * LANES, LANES))
        if block == inner:
            return even_edge[at], odd_edge[at]
        return even[at], odd[at]

    def combine(even, odd, start, pair, block):
        own = [part(even, odd, k, pair, block) for k in range(4)]
        bottom = own[0][0] + own[0][1]
        top = own[0][0] - own[0][1]
        e, o = part(even, odd, 0, pair, (block - 1) % blocks)
        before = pltpu.roll(jnp.where(lane == LANES - 1, e - o, top), 1, 1)
        e, o = part(even, odd, 0, pair, (block + 1) % blocks)
        after = pltpu.roll(jnp.where(lane == 0, e + o, bottom), LANES - 1, 1)
        if block == 0:
            before = jnp.where(is_first, bottom, before)
        if block == inner - 1:
            after = jnp.where(is_last, top, after)
        change = [None] * 8
        change[0] = bottom + before
        change[7] = top + after
        for k in range(1, 4):
            change[k] = own[k][0] + own[k][1]
            change[7 - k] = own[k][0] - own[k][1]
        return [slab(start, a, pair, block % inner) + change[a] for a in range(8)]

    def carry_edge(t, pair):
        carry(
            from_even,
            from_odd,
            t,
            [slab(v_edge, a, pair, 0) for a in range(8)],
            adv_edge,
            high_edge,
            low_edge,
            pair,
            0,
        )

    for pair in range(4):
        carry_edge([slab(t_edge, a, pair, 0) for a in range(8)], pair)
    smooth(smoothing, high_edge, low_edge, even_edge, odd_edge, [0])
    for group in groups:
        for pair in range(4):
            for block in group:
                carry(
                    from_even,
                    from_odd,
                    combine(even_first, odd_first, adv, pair, block),
                    [slab(v, a, pair, block) for a in range(8)],
                    adv_second,
                    high,
                    low,
                    pair,
                    block,
                )
        smooth(smoothing, high, low, even_second, odd_second, group)
    for pair in range(4):
        carry_edge(combine(even_first, odd_first, adv_edge, pair, inner), pair)
    smooth(smoothing, high_edge, low_edge, even_edge, odd_edge, [0])
    stores = []
    for number, group in enumerate(groups):
        for block in group:
            lanes = pl.ds(block * LANES, LANES)
            for pair in range(4):
                t = combine(even_second, odd_second, adv_second, pair, block)
                for a in range(8):
                    t_new[a, pl.ds(2 * pair, 2), :, lanes] = t[a].reshape(2, 8, LANES)
            for side in range(2):
                own = t_new[:, 7 * side, :, lanes].reshape(64, LANES)
                wall[pl.ds(64 * side, 64), lanes] = own
                layer = film[pl.ds(64 * side, 64), lanes]
                faces[side, lanes, :] = jnp.concatenate([layer, layer * own], axis=0).T
        lanes = pl.ds(group[0] * LANES, 2 * LANES)
        copy = pltpu.make_async_copy(
            t_new.at[:, :, :, lanes], t_out.at[:, :, :, lanes], out_sems.at[number]
        )
        copy.start()
        stores.append(copy)
    copy = pltpu.make_async_copy(wall, wall_out, out_sems.at[4])
    copy.start()
    stores.append(copy)
    position_copy.wait()

    def scatter(i, _):
        for j in range(128):
            spot = position[i, j]
            sending[pl.ds(spot, 1), :] = faces[j % 2, pl.ds(i * 64 + j // 2, 1), :]
        return 0

    lax.fori_loop(0, 16, scatter, 0)
    for copy in stores:
        copy.wait()


def owner_kernel(
    arrived,
    cell,
    plate_in,
    conductivity_in,
    plate_op_in,
    sheet_out,
    returning,
    hot,
    parts,
    plate,
    conductivity,
    plate_op,
    sheet,
    in_sems,
    out_sem,
):
    loads = [
        pltpu.make_async_copy(plate_in, plate, in_sems.at[0]),
        pltpu.make_async_copy(conductivity_in, conductivity, in_sems.at[1]),
        pltpu.make_async_copy(plate_op_in, plate_op, in_sems.at[2]),
    ]
    for copy in loads:
        copy.start()
    name = lax.broadcasted_iota(jnp.int32, (512, LANES), 0)
    both = 0.0
    for chunk in range(4):
        for i in range(8):
            place = 8 * chunk + i
            block = arrived[
                pl.ds(8 * (place % 16), 8), pl.ds(16 * (place // 16), 16), :
            ].reshape(128, LANES)
            first, second = halves(block)
            rows = pl.ds(place * 128, 128)
            parts[rows, pl.ds(0, LANES)] = first
            parts[rows, pl.ds(LANES, LANES)] = second
            hot[:, rows] = (
                (name == cell[place : place + 1, :]).astype(jnp.float32).astype(jnp.bfloat16)
            )
        slots = pl.ds(1024 * chunk, 1024)
        both = both + dot32(hot[:, slots], parts[slots, :])
    total = (both[:, :LANES] + both[:, LANES:]).T
    film_sum = total[:64]
    heat_sum = total[64:]
    for copy in loads:
        copy.wait()
    contact = (plate[0:64, :] + CONTACT * heat_sum) / (1.0 + CONTACT * film_sum)
    relaxed = jnp.concatenate([contact, plate[64:128, :]], axis=0)
    first, second = halves(relaxed)
    op_first = plate_op[:, pl.ds(0, 128)]
    op_second = plate_op[:, pl.ds(128, 128)]
    spread = dot32(op_first, first) + dot32(op_second, first) + dot32(op_first, second)
    conducted = relaxed + DT_PLATE * conductivity[...] * spread
    sheet[...] = conducted
    store = pltpu.make_async_copy(sheet, sheet_out, out_sem)
    store.start()
    first, second = halves(conducted[:64])
    mixed = jnp.concatenate([first, second], axis=0)
    for i in range(16):
        low = dot32(mixed, hot[:, pl.ds(i * 128, 128)])
        high = dot32(mixed, hot[:, pl.ds(2048 + i * 128, 128)])
        block = jnp.concatenate([low[:64] + low[64:], high[:64] + high[64:]], axis=0)
        returning[pl.ds(i * 128, 128), :] = block.T
    store.wait()


def finish_kernel(
    returned,
    position_in,
    film_in,
    wall_in,
    t_in,
    t_out,
    contact_out,
    position,
    film,
    wall,
    rows,
    gathered,
    contact,
    out,
    in_sems,
    out_sems,
):
    del t_in
    loads = [
        pltpu.make_async_copy(position_in, position, in_sems.at[0]),
        pltpu.make_async_copy(film_in, film, in_sems.at[1]),
        pltpu.make_async_copy(wall_in, wall, in_sems.at[2]),
    ]
    for copy in loads:
        copy.start()
    lane = lax.broadcasted_iota(jnp.int32, (16, LANES), 1)

    def expand(i, _):
        for k in range(8):
            block = returned[pl.ds(128 * i + 16 * k, 16), :]
            turned = pltpu.roll(block, 64, 1)
            at = 256 * i + 32 * k
            rows[pl.ds(at, 16), :] = jnp.where(lane < 64, block, turned)
            rows[pl.ds(at + 16, 16), :] = jnp.where(lane < 64, turned, block)
        return 0

    lax.fori_loop(0, 16, expand, 0)
    loads[0].wait()
    one = lax.broadcasted_iota(jnp.int32, (1, LANES), 1)
    stores = []
    for block in range(8):

        def gather(i, _):
            for j in range(64):
                low = rows[pl.ds(position[2 * block + i, 2 * j], 1), :]
                high = rows[pl.ds(position[2 * block + i, 2 * j + 1], 1), :]
                gathered[pl.ds(i * 64 + j, 1), :] = jnp.where(one < 64, low, high)
            return 0

        lax.fori_loop(0, 2, gather, 0)
        if block == 0:
            loads[1].wait()
            loads[2].wait()
        lanes = pl.ds(block * LANES, LANES)
        seen = gathered[...].T
        contact[:, lanes] = seen
        own = wall[:, lanes]
        out[:, :, :, lanes] = (
            own + MIXING_WEIGHT * (film[:, lanes] * (seen - own))
        ).reshape(2, 8, 8, LANES)
        copies = [
            pltpu.make_async_copy(
                contact.at[:, lanes], contact_out.at[:, lanes], out_sems.at[block, 0]
            )
        ] + [
            pltpu.make_async_copy(
                out.at[side, :, :, lanes], t_out.at[:, 7 * side, :, lanes], out_sems.at[block, 1 + side]
            )
            for side in range(2)
        ]
        for copy in copies:
            copy.start()
        stores += copies
    for copy in stores:
        copy.wait()


def vmem():
    return pl.BlockSpec(memory_space=pltpu.VMEM)


def smem():
    return pl.BlockSpec(memory_space=pltpu.SMEM)


def hbm():
    return pl.BlockSpec(memory_space=pltpu.HBM)


def far(array):
    return pltpu.with_memory_space_constraint(array, pltpu.HBM)


def params(mebibytes):
    return pltpu.CompilerParams(vmem_limit_bytes=mebibytes * 1024 * 1024)


def edges(warmth, velocity):
    side = jax.ShapeDtypeStruct((8, 512), jnp.float32)
    return pl.pallas_call(
        edge_kernel,
        out_shape=(side, side),
        in_specs=[hbm(), hbm()],
        out_specs=(vmem(), vmem()),
        scratch_shapes=[
            pltpu.VMEM((2, 2, 512, LANES), jnp.float32),
            pltpu.SemaphoreType.DMA((2, 2)),
        ],
        compiler_params=params(4),
        name="edges",
    )(far(warmth), far(velocity))


def begin(warmth, velocity, wall_film, owner):
    f32 = jnp.float32
    from_even, from_odd, smoothing, _ = gll_tables()
    count = warmth.shape[1]
    return pl.pallas_call(
        functools.partial(begin_kernel, from_even, from_odd),
        out_shape=(
            pltpu.VMEM((8, 8, 8, count), f32),
            pltpu.VMEM((8, 8, 8, count), f32),
            pltpu.VMEM((256, count), f32),
            pltpu.VMEM((256, count), f32),
            pltpu.VMEM((128, count), f32),
            pltpu.VMEM((2, 256, 512), jnp.bfloat16),
            jax.ShapeDtypeStruct((16, 128), jnp.int32),
        ),
        in_specs=[hbm(), hbm(), hbm(), hbm(), vmem()],
        out_specs=(vmem(),) * 7,
        scratch_shapes=[
            pltpu.VMEM((8, 8, 8, count), f32),
            pltpu.VMEM((512, count), jnp.bfloat16),
            pltpu.VMEM((512, count), jnp.bfloat16),
            pltpu.SemaphoreType.DMA((2, 5)),
        ],
        compiler_params=params(20),
        name="begin",
    )(
        far(warmth.reshape(8, 8, 8, count)),
        far(velocity.reshape(8, 8, 8, count)),
        far(wall_film),
        far(jnp.asarray(smoothing)),
        owner,
    )


def sweeps(v, adv, even, odd, film, smoothing, from_prev, from_next, position):
    f32 = jnp.float32
    bf16 = jnp.bfloat16
    from_even, from_odd, _, _ = gll_tables()
    count = v.shape[-1]
    near = [pltpu.with_memory_space_constraint(x, pltpu.VMEM) for x in (v, adv, even, odd, film, smoothing)]
    return pl.pallas_call(
        functools.partial(sweep_kernel, from_even, from_odd),
        out_shape=(
            jax.ShapeDtypeStruct((8, 8, 8, count), f32),
            pltpu.HBM((128, count), f32),
            jax.ShapeDtypeStruct((4096, LANES), f32),
        ),
        in_specs=[vmem()] * 8 + [hbm()],
        out_specs=(hbm(), hbm(), vmem()),
        scratch_shapes=[
            pltpu.SMEM((16, 128), jnp.int32),
            pltpu.VMEM((128, count), f32),
            pltpu.VMEM((8, 8, 8, LANES), f32),
            pltpu.VMEM((8, 8, 8, LANES), f32),
            pltpu.VMEM((8, 8, 8, LANES), f32),
            pltpu.VMEM((512, LANES), bf16),
            pltpu.VMEM((512, LANES), bf16),
            pltpu.VMEM((256, LANES), f32),
            pltpu.VMEM((256, LANES), f32),
            pltpu.VMEM((8, 8, 8, count), f32),
            pltpu.VMEM((8, 8, 8, count), f32),
            pltpu.VMEM((512, count), bf16),
            pltpu.VMEM((512, count), bf16),
            pltpu.VMEM((256, count), f32),
            pltpu.VMEM((256, count), f32),
            pltpu.VMEM((128, 512), f32),
            pltpu.VMEM((2, count, LANES), f32),
            pltpu.SemaphoreType.DMA(()),
            pltpu.SemaphoreType.DMA((5,)),
        ],
        compiler_params=params(28),
        name="sweeps",
    )(*near, from_prev, from_next, position)


def plates(arrived, cell, plate_temp, conductivity):
    f32 = jnp.float32
    plate_op = gll_tables()[3]
    return pl.pallas_call(
        owner_kernel,
        out_shape=(
            jax.ShapeDtypeStruct((128, 512), f32),
            jax.ShapeDtypeStruct((2048, LANES), f32),
        ),
        in_specs=[vmem(), vmem(), hbm(), hbm(), hbm()],
        out_specs=(hbm(), vmem()),
        scratch_shapes=[
            pltpu.VMEM((512, 4096), jnp.bfloat16),
            pltpu.VMEM((4096, 256), jnp.bfloat16),
            pltpu.VMEM((128, 512), f32),
            pltpu.VMEM((128, 512), f32),
            pltpu.VMEM((128, 256), jnp.bfloat16),
            pltpu.VMEM((128, 512), f32),
            pltpu.SemaphoreType.DMA((3,)),
            pltpu.SemaphoreType.DMA(()),
        ],
        compiler_params=params(20),
        name="plates",
    )(arrived, cell, far(plate_temp), far(conductivity), far(jnp.asarray(plate_op)))


def finish(returned, position, wall_film, wall, t_new):
    f32 = jnp.float32
    count = wall.shape[1]
    return pl.pallas_call(
        finish_kernel,
        out_shape=(
            jax.ShapeDtypeStruct((8, 8, 8, count), f32),
            jax.ShapeDtypeStruct((128, count), f32),
        ),
        in_specs=[vmem(), hbm(), hbm(), hbm(), hbm()],
        out_specs=(hbm(), hbm()),
        scratch_shapes=[
            pltpu.SMEM((16, 128), jnp.int32),
            pltpu.VMEM((128, count), f32),
            pltpu.VMEM((128, count), f32),
            pltpu.VMEM((4096, LANES), f32),
            pltpu.VMEM((LANES, LANES), f32),
            pltpu.VMEM((128, count), f32),
            pltpu.VMEM((2, 8, 8, count), f32),
            pltpu.SemaphoreType.DMA((3,)),
            pltpu.SemaphoreType.DMA((8, 3)),
        ],
        input_output_aliases={4: 0},
        compiler_params=params(12),
        name="finish",
    )(returned, far(position), far(wall_film), far(wall), t_new)


def shards(warmth, velocity, wall_film, face_owner, plate_temp, conductivity, plate_cell):
    count = warmth.shape[1]
    axes = ("flow", "grp")
    devices = lax.axis_size(axes)

    def exchange(rows):
        return lax.all_to_all(rows, axes, split_axis=0, concat_axis=0, tiled=True)

    to_next, to_prev = edges(warmth, velocity)
    up = [(i, i + 1) for i in range(devices - 1)]
    down = [(j, i) for i, j in up]
    from_prev = lax.ppermute(to_next, axes, up)
    from_next = lax.ppermute(to_prev, axes, down)
    *started, position = begin(warmth, velocity, wall_film, face_owner.reshape(16, 128))
    t_new, wall, sending = sweeps(*started, from_prev, from_next, position)
    cell = plate_cell.reshape(128, 2, 16).transpose(1, 0, 2).reshape(32, LANES)
    cell, sending = lax.optimization_barrier((cell, sending))
    arrived = exchange(sending.reshape(128, 32, LANES))
    sheet, returning = plates(arrived, cell, plate_temp, conductivity)
    returned = exchange(returning.reshape(128, 16, LANES)).reshape(2048, LANES)
    coolant, boundary = finish(returned, position, wall_film, wall, t_new)
    return coolant.reshape(512, count), boundary, sheet


def solution(mesh):
    placed = (
        P(None, ("flow", "grp")),
        P(None, ("flow", "grp")),
        P(None, ("flow", "grp")),
        P(("flow", "grp"), None),
        P(None, ("flow", "grp")),
        P(None, ("flow", "grp")),
        P(("flow", "grp")),
    )
    return jax.shard_map(
        shards,
        mesh=mesh,
        in_specs=placed,
        out_specs=(P(None, ("flow", "grp")), P(None, ("flow", "grp")), P(None, ("flow", "grp"))),
        check_vma=False,
    )
```

time: 106 us -> 95.1 us (0.90)
  blocking collectives: 24.5 us -> 63.6 us
  waiting for transfers between devices: 30 us -> 0.01 us
  starting transfers between devices: 19.8 us -> 7.7 us
  Pallas kernels: 27 us -> 22.3 us
  local copies, waits for them, and re-layouts: 2.86 us -> 0.33 us
    all_to_all x1 -> x2, blocking collectives: 24.5 us -> 63.6 us  [exchange(): return lax.all_to_all(rows, axes, split_axis=0, concat_axis=0, tiled=True)]
    all_to_all x1 -> x0, waiting for transfers between devices: 30 us -> none  [shards(): lax.all_to_all(sending.reshape(128, 32, LANES), axes, split_axis=0, conca...]
    all_to_all x1 -> x0, starting transfers between devices: 12.1 us -> none  [shards(): lax.all_to_all(sending.reshape(128, 32, LANES), axes, split_axis=0, conca...]
    pallas_call x5, Pallas kernels: 27 us -> 22.3 us  [the longest x1 6.1 us: sweeps(): pl.pallas_call(functools.partial(sweep_kernel, from_even, from_odd), out_...]
    unnamed x8 -> x6, local copies, waits for them, and re-layouts: 1.94 us -> 0.01 us
  transfers between devices with their start and end apart: 3 -> 2, of which waited for: 1 -> 0; matrix products, arithmetic and copies ran while one was open for 1% -> 0% of each run, Pallas kernels for 2% -> 4%
where the time goes in v1:
time: 95.1 us; the launch traced here: 94.9 us
  blocking collectives  63.6 us (67%)
  Pallas kernels  22.3 us (23%)
  starting transfers between devices  7.7 us (8%)
    all_to_all x2, blocking collectives, exchange(): return lax.all_to_all(rows, axes, split_axis=0, concat_axis=0, tiled=True)  63.6 us
    pallas_call x1, Pallas kernels, sweeps(): pl.pallas_call(functools.partial(sweep_kernel, from_even, from_odd), out_...  6.1 us
    pallas_call x1, Pallas kernels, plates(): pl.pallas_call(owner_kernel, out_shape=(jax.ShapeDtypeStruct((128, 512),...  5.92 us
    pallas_call x1, Pallas kernels, finish(): pl.pallas_call(finish_kernel, out_shape=(jax.ShapeDtypeStruct((8, 8, 8, c...  4.77 us
    pallas_call x1, Pallas kernels, begin(): pl.pallas_call(functools.partial(begin_kernel, from_even, from_odd), out_...  3.97 us
    ppermute x1, starting transfers between devices, shards(): from_prev = lax.ppermute(to_next, axes, up)  3.95 us
    ppermute x1, starting transfers between devices, shards(): from_next = lax.ppermute(to_prev, axes, down)  3.75 us
  transfers between devices with their start and end apart: 2, of which 0 were waited for; matrix products, arithmetic and copies ran while one was open for 0% of the time, Pallas kernels for 4%

profile of v1, /device:TPU:1, one launch (start us, length us, event | category | flops | bytes accessed | tf_op | source)
XLA Modules:
  0.0 94.9 jit_solution(9198210116258523179)
XLA Ops:
  0.6 0.0 copy-start.2
  0.6 0.0 copy-start.1
  0.7 1.6 %edges.1 = (f32[8,512]{1,0:T(8,128)S(1)}, f32[8,512]{1,0:T(8,128)S(1)}) custom-call(f32[512,1024]{1,0:T(8,128)} %t_in.1, f32[512,1024]{1,0:T(8,128)} %v_in.1), custom_call_target="tpu_custom_call" | custom-call | tf_op jit(solution)/shard_map/edges/pallas_call | solution.py:554
  2.2 3.9 %collective-permute-start = (f32[8,512]{1,0:T(8,128)S(1)}, f32[8,512]{1,0:T(8,128)S(1)}, u32[]{:S(2)}, u32[]{:S(2)}) collective-permute-start(f32[8,512]{1,0:T(8,128)S(1)} %get-tuple-element.27), channel_id=1, source_target_pairs={{0,1},{1,2},{2,3},{3,4},{4,5},{5,6},{6,7},{7,8},{8,9},{9,10},{10,1... | collective-permute-start | bytes 49160 | tf_op jit(solution)/shard_map/ppermute | solution.py:708
  6.2 3.7 %collective-permute-start.1 = (f32[8,512]{1,0:T(8,128)S(1)}, f32[8,512]{1,0:T(8,128)S(1)}, u32[]{:S(2)}, u32[]{:S(2)}) collective-permute-start(f32[8,512]{1,0:T(8,128)S(1)} %get-tuple-element.28), channel_id=1, source_target_pairs={{1,0},{2,1},{3,2},{4,3},{5,4},{6,5},{7,6},{8,7},{9,8},{10,9},{11,1... | collective-permute-start | bytes 49160 | tf_op jit(solution)/shard_map/ppermute | solution.py:709
  10.0 0.0 copy-done.2
  10.0 0.2 reshape.33
  10.2 0.1 reshape.34.cell
  10.3 0.0 copy-done.1
  10.3 4.0 %begin.1 = (f32[8,8,8,1024]{3,2,1,0:T(8,128)S(1)}, f32[8,8,8,1024]{3,2,1,0:T(8,128)S(1)}, f32[256,1024]{1,0:T(8,128)S(1)}, f32[256,1024]{1,0:T(8,128)S(1)}, f32[...) custom-call(f32[8,8,8,1024]{3,2,1,0:T(8,128)} %bitcast.12, ...), custom_call_target="tpu_custom_call" | custom-call | tf_op jit(solution)/shard_map/begin/pallas_call | solution.py:572
  14.3 0.0 copy-start
  14.3 0.0 collective-permute-done.from_prev
  14.3 0.0 collective-permute-done.1.from_next
  14.3 6.1 %sweeps.1 = (f32[8,8,8,1024]{3,2,1,0:T(8,128)}, f32[128,1024]{1,0:T(8,128)}, f32[4096,128]{1,0:T(8,128)S(1)}) custom-call(f32[8,8,8,1024]{3,2,1,0:T(8,128)S(1)} %get-tuple-element.21.v, f32[8,8,8,1024]{3,2,1,0:T(8,128)S(1)} %get-tuple-element.22.adv, f32[256,1024]{1,0:T(8,128)S(1)} %get-tuple-element.23.even_first, ...), custom_call_target="tpu_custom_call" | custom-call | tf_op jit(solution)/shard_map/sweeps/pallas_call | solution.py:608
  20.4 0.0 copy-done
  20.4 40.7 %all_to_all.10.arrived = f32[128,32,128]{2,1,0:T(8,128)S(1)} all-to-all(f32[128,32,128]{2,1,0:T(8,128)S(1)} %bitcast.9), channel_id=1, replica_groups=mesh['flow'=32,'grp'=4] {'flow','grp'}, dimensions={0} | all-to-all | bytes 4194304 | tf_op jit(solution)/shard_map/all_to_all | solution.py:703
  61.1 5.9 %plates.1 = (f32[128,512]{1,0:T(8,128)}, f32[2048,128]{1,0:T(8,128)S(1)}) custom-call(f32[128,32,128]{2,1,0:T(8,128)S(1)} %all_to_all.10.arrived, s32[32,128]{1,0:T(8,128)S(1)} %reshape.34.cell, f32[128,512]{1,0:T(8,128)} %plate_in.1, f32[128,512]{1,0:T(8,128)} %conductivity_in.1, bf16[128,256]{1,0:T(8,128)(2,1)} %constant.5.clone.plate_op_in), custom_call_target="tpu_custom_call" | custom-call | tf_op jit(solution)/shard_map/plates/pallas_call | solution.py:646
  67.1 22.9 %all_to_all.11 = f32[128,16,128]{2,1,0:T(8,128)S(1)} all-to-all(f32[128,16,128]{2,1,0:T(8,128)S(1)} %bitcast.10), channel_id=1, replica_groups=mesh['flow'=32,'grp'=4] {'flow','grp'}, dimensions={0} | all-to-all | bytes 2097152 | tf_op jit(solution)/shard_map/all_to_all | solution.py:703
  90.0 4.8 %finish.1 = (f32[8,8,8,1024]{3,2,1,0:T(8,128)}, f32[128,1024]{1,0:T(8,128)}) custom-call(f32[2048,128]{1,0:T(8,128)S(1)} %bitcast.8, s32[16,128]{1,0:T(8,128)} %copy-done, f32[128,1024]{1,0:T(8,128)} %film_in.3, f32[128,1024]{1,0:T(8,128)} %get-tuple-element.34.wall_in, f32[8,8,8,1024]{3,2,1,0:T(8,128)} %get-tuple-element.35.t_in), custom_call_target="tpu_custom_call", output_to_operand_aliasing={{0}: (4, {})} | custom-call | tf_op jit(solution)/shard_map/finish/pallas_call | solution.py:672
  (1 shorter events, 0.0 us)
Async XLA Ops:
  0.6 9.3 %copy-start.2 = (s32[4096]{0:T(1024)S(1)}, s32[4096]{0:T(1024)}, u32[]{:S(2)}) copy-start(s32[4096]{0:T(1024)} %param.15) | copy-start | bytes 49156
  0.6 9.7 %copy-start.1 = (s32[2048,1]{0,1:T(1,128)S(1)}, s32[2048,1]{0,1:T(1,128)}, u32[]{:S(2)}) copy-start(s32[2048,1]{0,1:T(1,128)} %param.12) | copy-start | bytes 24580
  2.2 12.1 %collective-permute-start = (f32[8,512]{1,0:T(8,128)S(1)}, f32[8,512]{1,0:T(8,128)S(1)}, u32[]{:S(2)}, u32[]{:S(2)}) collective-permute-start(f32[8,512]{1,0:T(8,128)S(1)} %get-tuple-element.27), channel_id=1, source_target_pairs={{0,1},{1,2},{2,3},{3,4},{4,5},{5,6},{6,7},{7,8},{8,9},{9,10},{10,1... | collective-permute-start | bytes 49160 | tf_op jit(solution)/shard_map/ppermute | solution.py:708
  6.2 8.1 %collective-permute-start.1 = (f32[8,512]{1,0:T(8,128)S(1)}, f32[8,512]{1,0:T(8,128)S(1)}, u32[]{:S(2)}, u32[]{:S(2)}) collective-permute-start(f32[8,512]{1,0:T(8,128)S(1)} %get-tuple-element.28), channel_id=1, source_target_pairs={{1,0},{2,1},{3,2},{4,3},{5,4},{6,5},{7,6},{8,7},{9,8},{10,9},{11,1... | collective-permute-start | bytes 49160 | tf_op jit(solution)/shard_map/ppermute | solution.py:709
  14.3 6.1 %copy-start = (s32[16,128]{1,0:T(8,128)}, s32[16,128]{1,0:T(8,128)S(1)}, u32[]{:S(2)}) copy-start(s32[16,128]{1,0:T(8,128)S(1)} %get-tuple-element.29.position_in) | copy-start | bytes 24580

commit v2 on v1

--- a/solution.py
+++ b/solution.py
@@ -145,20 +145,31 @@
             )
 
 
-def carry(from_even, from_odd, t, v, adv, high, low, pair, block):
-    at = pl.ds(2 * pair, 2)
+def carry(from_even, from_odd, start, v, adv, high, low, pair, block):
     lanes = pl.ds(block * LANES, LANES)
-    e = [t[k] + t[7 - k] for k in range(4)]
-    o = [t[k] - t[7 - k] for k in range(4)]
+    parts = []
+    for b in (2 * pair, 2 * pair + 1):
+        t = start(b)
+        e = [t[k] + t[7 - k] for k in range(4)]
+        o = [t[k] - t[7 - k] for k in range(4)]
+        kept = []
+        for i in range(4):
+            p = float(from_even[i, 0]) * e[0]
+            q = float(from_odd[i, 0]) * o[0]
+            for j in range(1, 4):
+                p = p + float(from_even[i, j]) * e[j]
+                q = q + float(from_odd[i, j]) * o[j]
+            near = t[i] + v[i, b, :, lanes] * (q + p)
+            far = t[7 - i] + v[7 - i, b, :, lanes] * (q - p)
+            adv[i, b, :, lanes] = near
+            adv[7 - i, b, :, lanes] = far
+            kept.append((near + far, near - far))
+        parts.append(kept)
     for i in range(4):
-        p = sum(float(from_even[i, j]) * e[j] for j in range(4))
-        q = sum(float(from_odd[i, j]) * o[j] for j in range(4))
-        near = t[i] + v[i] * (q + p)
-        far = t[7 - i] + v[7 - i] * (q - p)
-        adv[i, at, :, lanes] = near.reshape(2, 8, LANES)
-        adv[7 - i, at, :, lanes] = far.reshape(2, 8, LANES)
-        for number, part in enumerate((near + far, near - far)):
-            first, second = halves(part)
+        for number in range(2):
+            first, second = halves(
+                jnp.concatenate([parts[0][i][number], parts[1][i][number]], axis=0)
+            )
             rows = pl.ds(256 * number + 64 * i + 16 * pair, 16)
             high[rows, lanes] = first
             low[rows, lanes] = second
@@ -175,10 +186,6 @@
             + dot32(second, high[rows, lanes])
             + dot32(first, low[rows, lanes])
         )
-
-
-def slab(array, a, pair, block):
-    return array[a, pl.ds(2 * pair, 2), :, pl.ds(block * LANES, LANES)].reshape(16, LANES)
 
 
 def begin_kernel(
@@ -222,20 +229,23 @@
             copy.wait()
         for pair in range(4):
             for block in group:
+                lanes = pl.ds(block * LANES, LANES)
                 carry(
                     from_even,
                     from_odd,
-                    [slab(t, a, pair, block) for a in range(8)],
-                    [slab(v, a, pair, block) for a in range(8)],
+                    lambda b: [t[a, b, :, lanes] for a in range(8)],
+                    v,
                     adv,
                     high,
                     low,
                     pair,
                     block,
                 )
-        if number == 0:
+        if number > 0:
+            smooth(smoothing, high, low, even, odd, groups[number - 1])
+        else:
             smoothing_copy.wait()
-        smooth(smoothing, high, low, even, odd, group)
+    smooth(smoothing, high, low, even, odd, groups[-1])
     film_copy.wait()
 
 
@@ -286,101 +296,102 @@
         edge[126:128, :] = from_prev[pl.ds(2 * i, 2), :]
         array[...] = edge[...].T.reshape(8, 8, 8, LANES)
     sending[...] = jnp.zeros_like(sending)
-    lane = lax.broadcasted_iota(jnp.int32, (16, LANES), 1)
+    lane = lax.broadcasted_iota(jnp.int32, (8, LANES), 1)
     is_first = (lane == 0) & (from_prev[4:5, 0:LANES] == 0.0)
     is_last = (lane == LANES - 1) & (from_next[4:5, 0:LANES] == 0.0)
 
-    def part(even, odd, k, pair, block):
-        at = (pl.ds(64 * k + 16 * pair, 16), pl.ds((block % inner) * LANES, LANES))
+    changes = ((even_first, odd_first), (even_second, odd_second))
+
+    def part(sweep, k, b, block):
+        rows = pl.ds(64 * k + 8 * b, 8)
         if block == inner:
-            return even_edge[at], odd_edge[at]
-        return even[at], odd[at]
-
-    def combine(even, odd, start, pair, block):
-        own = [part(even, odd, k, pair, block) for k in range(4)]
-        bottom = own[0][0] + own[0][1]
-        top = own[0][0] - own[0][1]
-        e, o = part(even, odd, 0, pair, (block - 1) % blocks)
+            return even_edge[sweep, rows, :], odd_edge[sweep, rows, :]
+        even, odd = changes[sweep]
+        lanes = pl.ds(block * LANES, LANES)
+        return even[rows, lanes], odd[rows, lanes]
+
+    def combine(sweep, start, b, block):
+        e, o = part(sweep, 0, b, block)
+        bottom, top = e + o, e - o
+        e, o = part(sweep, 0, b, (block - 1) % blocks)
         before = pltpu.roll(jnp.where(lane == LANES - 1, e - o, top), 1, 1)
-        e, o = part(even, odd, 0, pair, (block + 1) % blocks)
+        e, o = part(sweep, 0, b, (block + 1) % blocks)
         after = pltpu.roll(jnp.where(lane == 0, e + o, bottom), LANES - 1, 1)
         if block == 0:
             before = jnp.where(is_first, bottom, before)
         if block == inner - 1:
             after = jnp.where(is_last, top, after)
-        change = [None] * 8
-        change[0] = bottom + before
-        change[7] = top + after
+        lanes = pl.ds((block % inner) * LANES, LANES)
+        t = [None] * 8
+        t[0] = start[0, b, :, lanes] + (bottom + before)
+        t[7] = start[7, b, :, lanes] + (top + after)
         for k in range(1, 4):
-            change[k] = own[k][0] + own[k][1]
-            change[7 - k] = own[k][0] - own[k][1]
-        return [slab(start, a, pair, block % inner) + change[a] for a in range(8)]
-
-    def carry_edge(t, pair):
-        carry(
-            from_even,
-            from_odd,
-            t,
-            [slab(v_edge, a, pair, 0) for a in range(8)],
-            adv_edge,
-            high_edge,
-            low_edge,
-            pair,
-            0,
+            e, o = part(sweep, k, b, block)
+            t[k] = start[k, b, :, lanes] + (e + o)
+            t[7 - k] = start[7 - k, b, :, lanes] + (e - o)
+        return t
+
+    def carry_edge(sweep, start):
+        into = adv_edge.at[sweep]
+        for pair in range(4):
+            carry(from_even, from_odd, start, v_edge, into, high_edge, low_edge, pair, 0)
+        smooth(
+            smoothing, high_edge, low_edge, even_edge.at[sweep], odd_edge.at[sweep], [0]
         )
 
-    for pair in range(4):
-        carry_edge([slab(t_edge, a, pair, 0) for a in range(8)], pair)
-    smooth(smoothing, high_edge, low_edge, even_edge, odd_edge, [0])
-    for group in groups:
+    def carry_inner(group):
         for pair in range(4):
             for block in group:
                 carry(
                     from_even,
                     from_odd,
-                    combine(even_first, odd_first, adv, pair, block),
-                    [slab(v, a, pair, block) for a in range(8)],
+                    functools.partial(combine, 0, adv, block=block),
+                    v,
                     adv_second,
                     high,
                     low,
                     pair,
                     block,
                 )
-        smooth(smoothing, high, low, even_second, odd_second, group)
-    for pair in range(4):
-        carry_edge(combine(even_first, odd_first, adv_edge, pair, inner), pair)
-    smooth(smoothing, high_edge, low_edge, even_edge, odd_edge, [0])
+
     stores = []
-    for number, group in enumerate(groups):
+
+    def complete(number):
+        group = groups[number]
         for block in group:
             lanes = pl.ds(block * LANES, LANES)
-            for pair in range(4):
-                t = combine(even_second, odd_second, adv_second, pair, block)
+            for b in range(8):
+                t = combine(1, adv_second, b, block)
                 for a in range(8):
-                    t_new[a, pl.ds(2 * pair, 2), :, lanes] = t[a].reshape(2, 8, LANES)
+                    t_new[a, b, :, lanes] = t[a]
             for side in range(2):
                 own = t_new[:, 7 * side, :, lanes].reshape(64, LANES)
                 wall[pl.ds(64 * side, 64), lanes] = own
                 layer = film[pl.ds(64 * side, 64), lanes]
                 faces[side, lanes, :] = jnp.concatenate([layer, layer * own], axis=0).T
+            for j in range(2 * LANES):
+                spot = position[2 * block + j // LANES, j % LANES]
+                sending[pl.ds(spot, 1), :] = faces[j % 2, pl.ds(block * LANES + j // 2, 1), :]
         lanes = pl.ds(group[0] * LANES, 2 * LANES)
         copy = pltpu.make_async_copy(
             t_new.at[:, :, :, lanes], t_out.at[:, :, :, lanes], out_sems.at[number]
         )
         copy.start()
         stores.append(copy)
+
+    carry_edge(0, lambda b: [t_edge[a, b, :, :] for a in range(8)])
+    carry_inner(groups[0])
+    carry_edge(1, functools.partial(combine, 0, adv_edge.at[0], block=inner))
+    position_copy.wait()
+    smooth(smoothing, high, low, even_second, odd_second, groups[0])
+    for number in range(1, len(groups)):
+        carry_inner(groups[number])
+        smooth(smoothing, high, low, even_second, odd_second, groups[number])
+        complete(number - 1)
+    complete(len(groups) - 1)
     copy = pltpu.make_async_copy(wall, wall_out, out_sems.at[4])
     copy.start()
     stores.append(copy)
-    position_copy.wait()
-
-    def scatter(i, _):
-        for j in range(128):
-            spot = position[i, j]
-            sending[pl.ds(spot, 1), :] = faces[j % 2, pl.ds(i * 64 + j // 2, 1), :]
-        return 0
-
-    lax.fori_loop(0, 16, scatter, 0)
     for copy in stores:
         copy.wait()
 
@@ -409,8 +420,9 @@
     ]
     for copy in loads:
         copy.start()
-    name = lax.broadcasted_iota(jnp.int32, (512, LANES), 0)
-    both = 0.0
+    name = lax.broadcasted_iota(jnp.int32, (512, LANES), 0).astype(jnp.int16)
+    one, zero = jnp.bfloat16(1), jnp.bfloat16(0)
+    both = [None, None]
     for chunk in range(4):
         for i in range(8):
             place = 8 * chunk + i
@@ -421,11 +433,14 @@
             rows = pl.ds(place * 128, 128)
             parts[rows, pl.ds(0, LANES)] = first
             parts[rows, pl.ds(LANES, LANES)] = second
-            hot[:, rows] = (
-                (name == cell[place : place + 1, :]).astype(jnp.float32).astype(jnp.bfloat16)
+            hot[:, rows] = jnp.where(
+                name == cell[place : place + 1, :].astype(jnp.int16), one, zero
             )
         slots = pl.ds(1024 * chunk, 1024)
-        both = both + dot32(hot[:, slots], parts[slots, :])
+        for i in range(2):
+            share = dot32(hot[pl.ds(256 * i, 256), slots], parts[slots, :])
+            both[i] = share if chunk == 0 else both[i] + share
+    both = jnp.concatenate(both, axis=0)
     total = (both[:, :LANES] + both[:, LANES:]).T
     film_sum = total[:64]
     heat_sum = total[64:]
@@ -443,10 +458,12 @@
     store.start()
     first, second = halves(conducted[:64])
     mixed = jnp.concatenate([first, second], axis=0)
+    seen = dot32(mixed, hot[...])
+    seen = seen[:64] + seen[64:]
     for i in range(16):
-        low = dot32(mixed, hot[:, pl.ds(i * 128, 128)])
-        high = dot32(mixed, hot[:, pl.ds(2048 + i * 128, 128)])
-        block = jnp.concatenate([low[:64] + low[64:], high[:64] + high[64:]], axis=0)
+        block = jnp.concatenate(
+            [seen[:, i * 128 : (i + 1) * 128], seen[:, 2048 + i * 128 : 2048 + (i + 1) * 128]], axis=0
+        )
         returning[pl.ds(i * 128, 128), :] = block.T
     store.wait()
 
@@ -493,15 +510,11 @@
     one = lax.broadcasted_iota(jnp.int32, (1, LANES), 1)
     stores = []
     for block in range(8):
-
-        def gather(i, _):
-            for j in range(64):
-                low = rows[pl.ds(position[2 * block + i, 2 * j], 1), :]
-                high = rows[pl.ds(position[2 * block + i, 2 * j + 1], 1), :]
-                gathered[pl.ds(i * 64 + j, 1), :] = jnp.where(one < 64, low, high)
-            return 0
-
-        lax.fori_loop(0, 2, gather, 0)
+        for j in range(LANES):
+            i, k = 2 * block + j // 64, 2 * (j % 64)
+            low = rows[pl.ds(position[i, k], 1), :]
+            high = rows[pl.ds(position[i, k + 1], 1), :]
+            gathered[pl.ds(j, 1), :] = jnp.where(one < 64, low, high)
         if block == 0:
             loads[1].wait()
             loads[2].wait()
@@ -619,11 +632,11 @@
             pltpu.VMEM((128, count), f32),
             pltpu.VMEM((8, 8, 8, LANES), f32),
             pltpu.VMEM((8, 8, 8, LANES), f32),
-            pltpu.VMEM((8, 8, 8, LANES), f32),
+            pltpu.VMEM((2, 8, 8, 8, LANES), f32),
             pltpu.VMEM((512, LANES), bf16),
             pltpu.VMEM((512, LANES), bf16),
-            pltpu.VMEM((256, LANES), f32),
-            pltpu.VMEM((256, LANES), f32),
+            pltpu.VMEM((2, 256, LANES), f32),
+            pltpu.VMEM((2, 256, LANES), f32),
             pltpu.VMEM((8, 8, 8, count), f32),
             pltpu.VMEM((8, 8, 8, count), f32),
             pltpu.VMEM((512, count), bf16),

time: 95.1 us -> 90.9 us (0.956)
  Pallas kernels: 22.3 us -> 18.3 us
    pallas_call x1, Pallas kernels: 5.92 us -> 3.41 us  [plates(): pl.pallas_call(owner_kernel, out_shape=(jax.ShapeDtypeStruct((128, 512),...]
    pallas_call x1, Pallas kernels: 4.77 us -> 3.76 us  [finish(): pl.pallas_call(finish_kernel, out_shape=(jax.ShapeDtypeStruct((8, 8, 8, c...]
where the time goes in v2:
time: 90.9 us; the launch traced here: 90.7 us
  blocking collectives  63.6 us (70%)
  Pallas kernels  18.3 us (20%)
  starting transfers between devices  7.7 us (8%)
    all_to_all x2, blocking collectives, exchange(): return lax.all_to_all(rows, axes, split_axis=0, concat_axis=0, tiled=True)  63.6 us
    pallas_call x1, Pallas kernels, sweeps(): pl.pallas_call(functools.partial(sweep_kernel, from_even, from_odd), out_...  5.59 us
    pallas_call x1, Pallas kernels, begin(): pl.pallas_call(functools.partial(begin_kernel, from_even, from_odd), out_...  3.98 us
    ppermute x1, starting transfers between devices, shards(): from_prev = lax.ppermute(to_next, axes, up)  3.95 us
    pallas_call x1, Pallas kernels, finish(): pl.pallas_call(finish_kernel, out_shape=(jax.ShapeDtypeStruct((8, 8, 8, c...  3.76 us
    ppermute x1, starting transfers between devices, shards(): from_next = lax.ppermute(to_prev, axes, down)  3.75 us
    pallas_call x1, Pallas kernels, plates(): pl.pallas_call(owner_kernel, out_shape=(jax.ShapeDtypeStruct((128, 512),...  3.41 us
  transfers between devices with their start and end apart: 2, of which 0 were waited for; matrix products, arithmetic and copies ran while one was open for 0% of the time, Pallas kernels for 4%

profile of v2, /device:TPU:1, one launch (start us, length us, event | category | flops | bytes accessed | tf_op | source)
XLA Modules:
  0.0 90.7 jit_solution(11381923391461157378)
XLA Ops:
  0.6 0.0 copy-start.2
  0.6 0.0 copy-start.1
  0.7 1.6 %edges.1 = (f32[8,512]{1,0:T(8,128)S(1)}, f32[8,512]{1,0:T(8,128)S(1)}) custom-call(f32[512,1024]{1,0:T(8,128)} %t_in.1, f32[512,1024]{1,0:T(8,128)} %v_in.1), custom_call_target="tpu_custom_call" | custom-call | tf_op jit(solution)/shard_map/edges/pallas_call | solution.py:567
  2.2 3.9 %collective-permute-start = (f32[8,512]{1,0:T(8,128)S(1)}, f32[8,512]{1,0:T(8,128)S(1)}, u32[]{:S(2)}, u32[]{:S(2)}) collective-permute-start(f32[8,512]{1,0:T(8,128)S(1)} %get-tuple-element.27), channel_id=1, source_target_pairs={{0,1},{1,2},{2,3},{3,4},{4,5},{5,6},{6,7},{7,8},{8,9},{9,10},{10,1... | collective-permute-start | bytes 49160 | tf_op jit(solution)/shard_map/ppermute | solution.py:721
  6.2 3.7 %collective-permute-start.1 = (f32[8,512]{1,0:T(8,128)S(1)}, f32[8,512]{1,0:T(8,128)S(1)}, u32[]{:S(2)}, u32[]{:S(2)}) collective-permute-start(f32[8,512]{1,0:T(8,128)S(1)} %get-tuple-element.28), channel_id=1, source_target_pairs={{1,0},{2,1},{3,2},{4,3},{5,4},{6,5},{7,6},{8,7},{9,8},{10,9},{11,1... | collective-permute-start | bytes 49160 | tf_op jit(solution)/shard_map/ppermute | solution.py:722
  10.0 0.0 copy-done.2
  10.0 0.2 reshape.33
  10.2 0.1 reshape.34.cell
  10.3 0.0 copy-done.1
  10.3 4.0 %begin.1 = (f32[8,8,8,1024]{3,2,1,0:T(8,128)S(1)}, f32[8,8,8,1024]{3,2,1,0:T(8,128)S(1)}, f32[256,1024]{1,0:T(8,128)S(1)}, f32[256,1024]{1,0:T(8,128)S(1)}, f32[...) custom-call(f32[8,8,8,1024]{3,2,1,0:T(8,128)} %bitcast.12, ...), custom_call_target="tpu_custom_call" | custom-call | tf_op jit(solution)/shard_map/begin/pallas_call | solution.py:585
  14.3 0.0 copy-start
  14.3 0.0 collective-permute-done.from_prev
  14.3 0.0 collective-permute-done.1.from_next
  14.3 5.6 %sweeps.1 = (f32[8,8,8,1024]{3,2,1,0:T(8,128)}, f32[128,1024]{1,0:T(8,128)}, f32[4096,128]{1,0:T(8,128)S(1)}) custom-call(f32[8,8,8,1024]{3,2,1,0:T(8,128)S(1)} %get-tuple-element.21.v, f32[8,8,8,1024]{3,2,1,0:T(8,128)S(1)} %get-tuple-element.22.adv, f32[256,1024]{1,0:T(8,128)S(1)} %get-tuple-element.23.even_first, ...), custom_call_target="tpu_custom_call" | custom-call | tf_op jit(solution)/shard_map/sweeps/pallas_call | solution.py:621
  19.9 0.0 copy-done
  19.9 40.7 %all_to_all.10.arrived = f32[128,32,128]{2,1,0:T(8,128)S(1)} all-to-all(f32[128,32,128]{2,1,0:T(8,128)S(1)} %bitcast.9), channel_id=1, replica_groups=mesh['flow'=32,'grp'=4] {'flow','grp'}, dimensions={0} | all-to-all | bytes 4194304 | tf_op jit(solution)/shard_map/all_to_all | solution.py:716
  60.6 3.4 %plates.1 = (f32[128,512]{1,0:T(8,128)}, f32[2048,128]{1,0:T(8,128)S(1)}) custom-call(f32[128,32,128]{2,1,0:T(8,128)S(1)} %all_to_all.10.arrived, s32[32,128]{1,0:T(8,128)S(1)} %reshape.34.cell, f32[128,512]{1,0:T(8,128)} %plate_in.1, f32[128,512]{1,0:T(8,128)} %conductivity_in.1, bf16[128,256]{1,0:T(8,128)(2,1)} %constant.5.clone.plate_op_in), custom_call_target="tpu_custom_call" | custom-call | tf_op jit(solution)/shard_map/plates/pallas_call | solution.py:659
  64.0 22.9 %all_to_all.11 = f32[128,16,128]{2,1,0:T(8,128)S(1)} all-to-all(f32[128,16,128]{2,1,0:T(8,128)S(1)} %bitcast.10), channel_id=1, replica_groups=mesh['flow'=32,'grp'=4] {'flow','grp'}, dimensions={0} | all-to-all | bytes 2097152 | tf_op jit(solution)/shard_map/all_to_all | solution.py:716
  86.9 3.8 %finish.1 = (f32[8,8,8,1024]{3,2,1,0:T(8,128)}, f32[128,1024]{1,0:T(8,128)}) custom-call(f32[2048,128]{1,0:T(8,128)S(1)} %bitcast.8, s32[16,128]{1,0:T(8,128)} %copy-done, f32[128,1024]{1,0:T(8,128)} %film_in.3, f32[128,1024]{1,0:T(8,128)} %get-tuple-element.34.wall_in, f32[8,8,8,1024]{3,2,1,0:T(8,128)} %get-tuple-element.35.t_in), custom_call_target="tpu_custom_call", output_to_operand_aliasing={{0}: (4, {})} | custom-call | tf_op jit(solution)/shard_map/finish/pallas_call | solution.py:685
  (1 shorter events, 0.0 us)
Async XLA Ops:
  0.6 9.3 %copy-start.2 = (s32[4096]{0:T(1024)S(1)}, s32[4096]{0:T(1024)}, u32[]{:S(2)}) copy-start(s32[4096]{0:T(1024)} %param.15) | copy-start | bytes 49156
  0.6 9.7 %copy-start.1 = (s32[2048,1]{0,1:T(1,128)S(1)}, s32[2048,1]{0,1:T(1,128)}, u32[]{:S(2)}) copy-start(s32[2048,1]{0,1:T(1,128)} %param.12) | copy-start | bytes 24580
  2.2 12.1 %collective-permute-start = (f32[8,512]{1,0:T(8,128)S(1)}, f32[8,512]{1,0:T(8,128)S(1)}, u32[]{:S(2)}, u32[]{:S(2)}) collective-permute-start(f32[8,512]{1,0:T(8,128)S(1)} %get-tuple-element.27), channel_id=1, source_target_pairs={{0,1},{1,2},{2,3},{3,4},{4,5},{5,6},{6,7},{7,8},{8,9},{9,10},{10,1... | collective-permute-start | bytes 49160 | tf_op jit(solution)/shard_map/ppermute | solution.py:721
  6.2 8.1 %collective-permute-start.1 = (f32[8,512]{1,0:T(8,128)S(1)}, f32[8,512]{1,0:T(8,128)S(1)}, u32[]{:S(2)}, u32[]{:S(2)}) collective-permute-start(f32[8,512]{1,0:T(8,128)S(1)} %get-tuple-element.28), channel_id=1, source_target_pairs={{1,0},{2,1},{3,2},{4,3},{5,4},{6,5},{7,6},{8,7},{9,8},{10,9},{11,1... | collective-permute-start | bytes 49160 | tf_op jit(solution)/shard_map/ppermute | solution.py:722
  14.3 5.6 %copy-start = (s32[16,128]{1,0:T(8,128)}, s32[16,128]{1,0:T(8,128)S(1)}, u32[]{:S(2)}) copy-start(s32[16,128]{1,0:T(8,128)S(1)} %get-tuple-element.29.position_in) | copy-start | bytes 24580

commit v3 on v2

--- a/solution.py
+++ b/solution.py
@@ -103,7 +103,7 @@
     return jnp.dot(a, b, preferred_element_type=jnp.float32)
 
 
-def edge_kernel(t_in, v_in, to_next, to_prev, held, sems):
+def edge_kernel(t_in, v_in, to_first, to_second, held, sems):
     count = t_in.shape[1]
     copies = []
     for i, array in enumerate((t_in, v_in)):
@@ -115,11 +115,15 @@
             copies.append(copy)
     for copy in copies:
         copy.wait()
+    odd = lax.axis_index("grp") % 2 == 1
     for i in range(2):
-        to_prev[pl.ds(2 * i, 2), :] = held[i, 0].T[0:2, :]
-        to_next[pl.ds(2 * i, 2), :] = held[i, 1].T[126:128, :]
-    to_prev[4:8, :] = jnp.ones((4, 512), jnp.float32)
-    to_next[4:8, :] = jnp.ones((4, 512), jnp.float32)
+        rows = pl.ds(2 * i, 2)
+        bottom = held[i, 0].T[0:2, :]
+        top = held[i, 1].T[126:128, :]
+        to_first[rows, :] = jnp.where(odd, bottom, top)
+        to_second[rows, :] = jnp.where(odd, top, bottom)
+    to_first[4:8, :] = jnp.ones((4, 512), jnp.float32)
+    to_second[4:8, :] = jnp.ones((4, 512), jnp.float32)
 
 
 def fill_positions(owner, position):
@@ -191,7 +195,7 @@
 def begin_kernel(
     from_even,
     from_odd,
-    t_in,
+    t,
     v_in,
     film_in,
     smoothing_in,
@@ -203,30 +207,27 @@
     film,
     smoothing,
     position,
-    t,
     high,
     low,
     sems,
 ):
-    count = t_in.shape[-1]
+    count = t.shape[-1]
     groups = [[2 * i, 2 * i + 1] for i in range(count // LANES // 2)]
-    loads = []
+    smoothing_copy = pltpu.make_async_copy(smoothing_in, smoothing, sems.at[0])
+    film_copy = pltpu.make_async_copy(film_in, film, sems.at[1])
+    v_copies = []
     for number, group in enumerate(groups):
         lanes = pl.ds(group[0] * LANES, 2 * LANES)
-        loads.append(
-            (
-                pltpu.make_async_copy(t_in.at[:, :, :, lanes], t.at[:, :, :, lanes], sems.at[0, number]),
-                pltpu.make_async_copy(v_in.at[:, :, :, lanes], v.at[:, :, :, lanes], sems.at[1, number]),
+        v_copies.append(
+            pltpu.make_async_copy(
+                v_in.at[:, :, :, lanes], v.at[:, :, :, lanes], sems.at[2 + number]
             )
         )
-    smoothing_copy = pltpu.make_async_copy(smoothing_in, smoothing, sems.at[0, 4])
-    film_copy = pltpu.make_async_copy(film_in, film, sems.at[1, 4])
-    for copy in loads[0] + (smoothing_copy,) + sum(loads[1:], ()) + (film_copy,):
+    for copy in [v_copies[0], smoothing_copy] + v_copies[1:] + [film_copy]:
         copy.start()
     fill_positions(owner, position)
-    for number, group in enumerate(groups):
-        for copy in loads[number]:
-            copy.wait()
+
+    def advect(group):
         for pair in range(4):
             for block in group:
                 lanes = pl.ds(block * LANES, LANES)
@@ -241,10 +242,15 @@
                     pair,
                     block,
                 )
-        if number > 0:
-            smooth(smoothing, high, low, even, odd, groups[number - 1])
-        else:
-            smoothing_copy.wait()
+
+    v_copies[0].wait()
+    advect(groups[0])
+    smoothing_copy.wait()
+    for copy in v_copies[1:]:
+        copy.wait()
+    for number in range(1, len(groups)):
+        advect(groups[number])
+        smooth(smoothing, high, low, even, odd, groups[number - 1])
     smooth(smoothing, high, low, even, odd, groups[-1])
     film_copy.wait()
 
@@ -258,8 +264,8 @@
     odd_first,
     film,
     smoothing,
-    from_prev,
-    from_next,
+    from_first,
+    from_second,
     position_in,
     t_out,
     wall_out,
@@ -290,10 +296,13 @@
     inner = count // LANES
     blocks = inner + 1
     groups = [[2 * i, 2 * i + 1] for i in range(inner // 2)]
+    odd = lax.axis_index("grp") % 2 == 1
+    from_prev = jnp.where(odd, from_first[...], from_second[...])
+    from_next = jnp.where(odd, from_second[...], from_first[...])
     edge[...] = jnp.zeros_like(edge)
     for i, array in enumerate((t_edge, v_edge)):
-        edge[0:2, :] = from_next[pl.ds(2 * i, 2), :]
-        edge[126:128, :] = from_prev[pl.ds(2 * i, 2), :]
+        edge[0:2, :] = from_next[2 * i : 2 * i + 2, :]
+        edge[126:128, :] = from_prev[2 * i : 2 * i + 2, :]
         array[...] = edge[...].T.reshape(8, 8, 8, LANES)
     sending[...] = jnp.zeros_like(sending)
     lane = lax.broadcasted_iota(jnp.int32, (8, LANES), 1)
@@ -420,6 +429,16 @@
     ]
     for copy in loads:
         copy.start()
+    lane = lax.broadcasted_iota(jnp.int32, (16, LANES), 1)
+    cells = []
+    for half in range(2):
+        ordered = jnp.zeros((16, LANES), jnp.int32)
+        for i in range(8):
+            own = cell[pl.ds(i // 4, 16, stride=2), :]
+            shift = (16 * i - 32 * (i % 4) - 16 * half) % LANES
+            moved = pltpu.roll(own, shift, 1) if shift else own
+            ordered = jnp.where(lane // 16 == i, moved, ordered)
+        cells.append(ordered.astype(jnp.int16))
     name = lax.broadcasted_iota(jnp.int32, (512, LANES), 0).astype(jnp.int16)
     one, zero = jnp.bfloat16(1), jnp.bfloat16(0)
     both = [None, None]
@@ -434,7 +453,7 @@
             parts[rows, pl.ds(0, LANES)] = first
             parts[rows, pl.ds(LANES, LANES)] = second
             hot[:, rows] = jnp.where(
-                name == cell[place : place + 1, :].astype(jnp.int16), one, zero
+                name == cells[place // 16][place % 16 : place % 16 + 1, :], one, zero
             )
         slots = pl.ds(1024 * chunk, 1024)
         for i in range(2):
@@ -578,10 +597,14 @@
     )(far(warmth), far(velocity))
 
 
-def begin(warmth, velocity, wall_film, owner):
+def near(array):
+    return pltpu.with_memory_space_constraint(array, pltpu.VMEM)
+
+
+def begin(t, v, wall_film, owner):
     f32 = jnp.float32
     from_even, from_odd, smoothing, _ = gll_tables()
-    count = warmth.shape[1]
+    count = t.shape[-1]
     return pl.pallas_call(
         functools.partial(begin_kernel, from_even, from_odd),
         out_shape=(
@@ -593,23 +616,16 @@
             pltpu.VMEM((2, 256, 512), jnp.bfloat16),
             jax.ShapeDtypeStruct((16, 128), jnp.int32),
         ),
-        in_specs=[hbm(), hbm(), hbm(), hbm(), vmem()],
+        in_specs=[vmem(), hbm(), hbm(), hbm(), vmem()],
         out_specs=(vmem(),) * 7,
         scratch_shapes=[
-            pltpu.VMEM((8, 8, 8, count), f32),
             pltpu.VMEM((512, count), jnp.bfloat16),
             pltpu.VMEM((512, count), jnp.bfloat16),
-            pltpu.SemaphoreType.DMA((2, 5)),
+            pltpu.SemaphoreType.DMA((6,)),
         ],
         compiler_params=params(20),
         name="begin",
-    )(
-        far(warmth.reshape(8, 8, 8, count)),
-        far(velocity.reshape(8, 8, 8, count)),
-        far(wall_film),
-        far(jnp.asarray(smoothing)),
-        owner,
-    )
+    )(near(t), far(v), far(wall_film), far(jnp.asarray(smoothing)), owner)
 
 
 def sweeps(v, adv, even, odd, film, smoothing, from_prev, from_next, position):
@@ -617,7 +633,7 @@
     bf16 = jnp.bfloat16
     from_even, from_odd, _, _ = gll_tables()
     count = v.shape[-1]
-    near = [pltpu.with_memory_space_constraint(x, pltpu.VMEM) for x in (v, adv, even, odd, film, smoothing)]
+    held = [near(x) for x in (v, adv, even, odd, film, smoothing)]
     return pl.pallas_call(
         functools.partial(sweep_kernel, from_even, from_odd),
         out_shape=(
@@ -650,7 +666,7 @@
         ],
         compiler_params=params(28),
         name="sweeps",
-    )(*near, from_prev, from_next, position)
+    )(*held, from_prev, from_next, position)
 
 
 def plates(arrived, cell, plate_temp, conductivity):
@@ -688,7 +704,7 @@
             jax.ShapeDtypeStruct((8, 8, 8, count), f32),
             jax.ShapeDtypeStruct((128, count), f32),
         ),
-        in_specs=[vmem(), hbm(), hbm(), hbm(), hbm()],
+        in_specs=[vmem(), vmem(), hbm(), hbm(), hbm()],
         out_specs=(hbm(), hbm()),
         scratch_shapes=[
             pltpu.SMEM((16, 128), jnp.int32),
@@ -704,7 +720,7 @@
         input_output_aliases={4: 0},
         compiler_params=params(12),
         name="finish",
-    )(returned, far(position), far(wall_film), far(wall), t_new)
+    )(returned, near(position), far(wall_film), far(wall), t_new)
 
 
 def shards(warmth, velocity, wall_film, face_owner, plate_temp, conductivity, plate_cell):
@@ -715,15 +731,15 @@
     def exchange(rows):
         return lax.all_to_all(rows, axes, split_axis=0, concat_axis=0, tiled=True)
 
-    to_next, to_prev = edges(warmth, velocity)
-    up = [(i, i + 1) for i in range(devices - 1)]
-    down = [(j, i) for i, j in up]
-    from_prev = lax.ppermute(to_next, axes, up)
-    from_next = lax.ppermute(to_prev, axes, down)
-    *started, position = begin(warmth, velocity, wall_film, face_owner.reshape(16, 128))
-    t_new, wall, sending = sweeps(*started, from_prev, from_next, position)
-    cell = plate_cell.reshape(128, 2, 16).transpose(1, 0, 2).reshape(32, LANES)
-    cell, sending = lax.optimization_barrier((cell, sending))
+    to_first, to_second = edges(warmth, velocity)
+    pairs = [[(i, i + 1) for i in range(start, devices - 1, 2)] for start in (0, 1)]
+    swaps = [forth + [(j, i) for i, j in forth] for forth in pairs]
+    from_first = lax.ppermute(to_first, axes, swaps[0])
+    from_second = lax.ppermute(to_second, axes, swaps[1])
+    t, v = (x.reshape(8, 8, 8, count) for x in (warmth, velocity))
+    *started, position = begin(t, v, wall_film, face_owner.reshape(16, 128))
+    t_new, wall, sending = sweeps(*started, from_first, from_second, position)
+    cell = plate_cell.reshape(32, LANES)
     arrived = exchange(sending.reshape(128, 32, LANES))
     sheet, returning = plates(arrived, cell, plate_temp, conductivity)
     returned = exchange(returning.reshape(128, 16, LANES)).reshape(2048, LANES)

time: 90.9 us -> 89.6 us (0.986)
  starting transfers between devices: 7.7 us -> 6.67 us
    ppermute x2, starting transfers between devices: 7.7 us -> 6.67 us  [the longest x1 4.55 us: shards(): from_second = lax.ppermute(to_second, axes, swaps[1])]
where the time goes in v3:
time: 89.6 us; the launch traced here: 89.4 us
  blocking collectives  64.1 us (72%)
  Pallas kernels  17.9 us (20%)
  starting transfers between devices  6.67 us (7%)
    all_to_all x2, blocking collectives, exchange(): return lax.all_to_all(rows, axes, split_axis=0, concat_axis=0, tiled=True)  64.1 us
    pallas_call x1, Pallas kernels, sweeps(): pl.pallas_call(functools.partial(sweep_kernel, from_even, from_odd), out_...  5.61 us
    ppermute x1, starting transfers between devices, shards(): from_second = lax.ppermute(to_second, axes, swaps[1])  4.55 us
    pallas_call x1, Pallas kernels, finish(): pl.pallas_call(finish_kernel, out_shape=(jax.ShapeDtypeStruct((8, 8, 8, c...  3.76 us
    pallas_call x1, Pallas kernels, begin(): pl.pallas_call(functools.partial(begin_kernel, from_even, from_odd), out_...  3.46 us
    pallas_call x1, Pallas kernels, plates(): pl.pallas_call(owner_kernel, out_shape=(jax.ShapeDtypeStruct((128, 512),...  3.32 us
    ppermute x1, starting transfers between devices, shards(): from_first = lax.ppermute(to_first, axes, swaps[0])  2.12 us
  transfers between devices with their start and end apart: 2, of which 0 were waited for; matrix products, arithmetic and copies ran while one was open for 0% of the time, Pallas kernels for 4%

profile of v3, /device:TPU:1, one launch (start us, length us, event | category | flops | bytes accessed | tf_op | source)
XLA Modules:
  0.0 89.4 jit_solution(3834397210234307331)
XLA Ops:
  0.6 0.0 copy-start
  0.6 0.0 copy-start.2
  0.6 1.7 %edges.1 = (f32[8,512]{1,0:T(8,128)S(1)}, f32[8,512]{1,0:T(8,128)S(1)}) custom-call(f32[512,1024]{1,0:T(8,128)} %t_in.1, f32[512,1024]{1,0:T(8,128)} %v_in.1), custom_call_target="tpu_custom_call" | custom-call | tf_op jit(solution)/shard_map/edges/pallas_call | solution.py:586
  2.4 2.1 %collective-permute-start = (f32[8,512]{1,0:T(8,128)S(1)}, f32[8,512]{1,0:T(8,128)S(1)}, u32[]{:S(2)}, u32[]{:S(2)}) collective-permute-start(f32[8,512]{1,0:T(8,128)S(1)} %get-tuple-element.25), channel_id=1, source_target_pairs={{0,1},{2,3},{4,5},{6,7},{8,9},{10,11},{12,13},{14,15},{16,17},{18,... | collective-permute-start | bytes 49160 | tf_op jit(solution)/shard_map/ppermute | solution.py:737
  4.5 4.6 %collective-permute-start.1 = (f32[8,512]{1,0:T(8,128)S(1)}, f32[8,512]{1,0:T(8,128)S(1)}, u32[]{:S(2)}, u32[]{:S(2)}) collective-permute-start(f32[8,512]{1,0:T(8,128)S(1)} %get-tuple-element.26), channel_id=1, source_target_pairs={{1,2},{3,4},{5,6},{7,8},{9,10},{11,12},{13,14},{15,16},{17,18},{19... | collective-permute-start | bytes 49160 | tf_op jit(solution)/shard_map/ppermute | solution.py:738
  9.1 0.0 copy-done
  9.1 0.0 copy-done.2
  9.1 3.5 %begin.1 = (f32[8,8,8,1024]{3,2,1,0:T(8,128)S(1)}, f32[8,8,8,1024]{3,2,1,0:T(8,128)S(1)}, f32[256,1024]{1,0:T(8,128)S(1)}, f32[256,1024]{1,0:T(8,128)S(1)}, f32[...) custom-call(f32[8,8,8,1024]{3,2,1,0:T(8,128)S(1)} %bitcast.8, ...), custom_call_target="tpu_custom_call" | custom-call | tf_op jit(solution)/shard_map/begin/pallas_call | solution.py:608
  12.5 0.0 collective-permute-done.from_first
  12.6 0.0 collective-permute-done.1.from_second
  12.6 5.6 %sweeps.1 = (f32[8,8,8,1024]{3,2,1,0:T(8,128)}, f32[128,1024]{1,0:T(8,128)}, f32[4096,128]{1,0:T(8,128)S(1)}) custom-call(f32[8,8,8,1024]{3,2,1,0:T(8,128)S(1)} %get-tuple-element.19.v, f32[8,8,8,1024]{3,2,1,0:T(8,128)S(1)} %get-tuple-element.20.adv, f32[256,1024]{1,0:T(8,128)S(1)} %get-tuple-element.21.even_first, ...), custom_call_target="tpu_custom_call" | custom-call | tf_op jit(solution)/shard_map/sweeps/pallas_call | solution.py:637
  18.2 0.0 copy-start.1
  18.2 41.2 %all_to_all.10.arrived = f32[128,32,128]{2,1,0:T(8,128)S(1)} all-to-all(f32[128,32,128]{2,1,0:T(8,128)S(1)} %bitcast.10), channel_id=1, replica_groups=mesh['flow'=32,'grp'=4] {'flow','grp'}, dimensions={0} | all-to-all | bytes 4194304 | tf_op jit(solution)/shard_map/all_to_all | solution.py:732
  59.4 0.0 copy-done.1
  59.4 3.3 %plates.1 = (f32[128,512]{1,0:T(8,128)}, f32[2048,128]{1,0:T(8,128)S(1)}) custom-call(f32[128,32,128]{2,1,0:T(8,128)S(1)} %all_to_all.10.arrived, s32[32,128]{1,0:T(8,128)S(1)} %bitcast.12, f32[128,512]{1,0:T(8,128)} %plate_in.1, f32[128,512]{1,0:T(8,128)} %conductivity_in.1, bf16[128,256]{1,0:T(8,128)(2,1)} %constant.5.clone.plate_op_in), custom_call_target="tpu_custom_call" | custom-call | tf_op jit(solution)/shard_map/plates/pallas_call | solution.py:675
  62.7 22.9 %all_to_all.11 = f32[128,16,128]{2,1,0:T(8,128)S(1)} all-to-all(f32[128,16,128]{2,1,0:T(8,128)S(1)} %bitcast.11), channel_id=1, replica_groups=mesh['flow'=32,'grp'=4] {'flow','grp'}, dimensions={0} | all-to-all | bytes 2097152 | tf_op jit(solution)/shard_map/all_to_all | solution.py:732
  85.6 3.8 %finish.1 = (f32[8,8,8,1024]{3,2,1,0:T(8,128)}, f32[128,1024]{1,0:T(8,128)}) custom-call(f32[2048,128]{1,0:T(8,128)S(1)} %bitcast.9, s32[16,128]{1,0:T(8,128)S(1)} %get-tuple-element.27.position_in, f32[128,1024]{1,0:T(8,128)} %film_in.3, f32[128,1024]{1,0:T(8,128)} %get-tuple-element.30.wall_in, ...), custom_call_target="tpu_custom_call", output_to_operand_aliasing={{0}: (4, {})} | custom-call | tf_op jit(solution)/shard_map/finish/pallas_call | solution.py:701
Async XLA Ops:
  0.6 8.4 %copy-start = (f32[512,1024]{1,0:T(8,128)S(1)}, f32[512,1024]{1,0:T(8,128)}, u32[]{:S(2)}) copy-start(f32[512,1024]{1,0:T(8,128)} %t_in.1) | copy-start | bytes 6291460
  0.6 8.4 %copy-start.2 = (s32[2048,1]{0,1:T(1,128)S(1)}, s32[2048,1]{0,1:T(1,128)}, u32[]{:S(2)}) copy-start(s32[2048,1]{0,1:T(1,128)} %param.12) | copy-start | bytes 24580
  2.4 10.2 %collective-permute-start = (f32[8,512]{1,0:T(8,128)S(1)}, f32[8,512]{1,0:T(8,128)S(1)}, u32[]{:S(2)}, u32[]{:S(2)}) collective-permute-start(f32[8,512]{1,0:T(8,128)S(1)} %get-tuple-element.25), channel_id=1, source_target_pairs={{0,1},{2,3},{4,5},{6,7},{8,9},{10,11},{12,13},{14,15},{16,17},{18,... | collective-permute-start | bytes 49160 | tf_op jit(solution)/shard_map/ppermute | solution.py:737
  4.5 8.1 %collective-permute-start.1 = (f32[8,512]{1,0:T(8,128)S(1)}, f32[8,512]{1,0:T(8,128)S(1)}, u32[]{:S(2)}, u32[]{:S(2)}) collective-permute-start(f32[8,512]{1,0:T(8,128)S(1)} %get-tuple-element.26), channel_id=1, source_target_pairs={{1,2},{3,4},{5,6},{7,8},{9,10},{11,12},{13,14},{15,16},{17,18},{19... | collective-permute-start | bytes 49160 | tf_op jit(solution)/shard_map/ppermute | solution.py:738
  18.2 41.2 %copy-start.1 = (s32[4096]{0:T(1024)S(1)}, s32[4096]{0:T(1024)}, u32[]{:S(2)}) copy-start(s32[4096]{0:T(1024)} %param.15) | copy-start | bytes 49156

commit v4 on v3

--- a/solution.py
+++ b/solution.py
@@ -207,6 +207,7 @@
     film,
     smoothing,
     position,
+    cleared,
     high,
     low,
     sems,
@@ -225,6 +226,7 @@
         )
     for copy in [v_copies[0], smoothing_copy] + v_copies[1:] + [film_copy]:
         copy.start()
+    cleared[...] = jnp.zeros_like(cleared)
     fill_positions(owner, position)
 
     def advect(group):
@@ -267,6 +269,7 @@
     from_first,
     from_second,
     position_in,
+    cleared,
     t_out,
     wall_out,
     sending,
@@ -290,6 +293,7 @@
     in_sem,
     out_sems,
 ):
+    del cleared
     position_copy = pltpu.make_async_copy(position_in, position, in_sem)
     position_copy.start()
     count = v.shape[-1]
@@ -304,7 +308,6 @@
         edge[0:2, :] = from_next[2 * i : 2 * i + 2, :]
         edge[126:128, :] = from_prev[2 * i : 2 * i + 2, :]
         array[...] = edge[...].T.reshape(8, 8, 8, LANES)
-    sending[...] = jnp.zeros_like(sending)
     lane = lax.broadcasted_iota(jnp.int32, (8, LANES), 1)
     is_first = (lane == 0) & (from_prev[4:5, 0:LANES] == 0.0)
     is_last = (lane == LANES - 1) & (from_next[4:5, 0:LANES] == 0.0)
@@ -396,7 +399,9 @@
     for number in range(1, len(groups)):
         carry_inner(groups[number])
         smooth(smoothing, high, low, even_second, odd_second, groups[number])
-        complete(number - 1)
+        if number > 1:
+            complete(number - 2)
+    complete(len(groups) - 2)
     complete(len(groups) - 1)
     copy = pltpu.make_async_copy(wall, wall_out, out_sems.at[4])
     copy.start()
@@ -477,13 +482,15 @@
     store.start()
     first, second = halves(conducted[:64])
     mixed = jnp.concatenate([first, second], axis=0)
-    seen = dot32(mixed, hot[...])
-    seen = seen[:64] + seen[64:]
-    for i in range(16):
-        block = jnp.concatenate(
-            [seen[:, i * 128 : (i + 1) * 128], seen[:, 2048 + i * 128 : 2048 + (i + 1) * 128]], axis=0
-        )
-        returning[pl.ds(i * 128, 128), :] = block.T
+    for chunk in range(4):
+        seen = []
+        for half in range(2):
+            both_parts = dot32(mixed, hot[:, pl.ds(2048 * half + 512 * chunk, 512)])
+            seen.append(both_parts[:64] + both_parts[64:])
+        for i in range(4):
+            slots = slice(i * 128, (i + 1) * 128)
+            block = jnp.concatenate([seen[0][:, slots], seen[1][:, slots]], axis=0)
+            returning[pl.ds(512 * chunk + i * 128, 128), :] = block.T
     store.wait()
 
 
@@ -516,15 +523,15 @@
     lane = lax.broadcasted_iota(jnp.int32, (16, LANES), 1)
 
     def expand(i, _):
-        for k in range(8):
-            block = returned[pl.ds(128 * i + 16 * k, 16), :]
+        for k in range(32):
+            block = returned[pl.ds(512 * i + 16 * k, 16), :]
             turned = pltpu.roll(block, 64, 1)
-            at = 256 * i + 32 * k
+            at = 1024 * i + 32 * k
             rows[pl.ds(at, 16), :] = jnp.where(lane < 64, block, turned)
             rows[pl.ds(at + 16, 16), :] = jnp.where(lane < 64, turned, block)
         return 0
 
-    lax.fori_loop(0, 16, expand, 0)
+    lax.fori_loop(0, 4, expand, 0)
     loads[0].wait()
     one = lax.broadcasted_iota(jnp.int32, (1, LANES), 1)
     stores = []
@@ -615,9 +622,10 @@
             pltpu.VMEM((128, count), f32),
             pltpu.VMEM((2, 256, 512), jnp.bfloat16),
             jax.ShapeDtypeStruct((16, 128), jnp.int32),
+            pltpu.VMEM((4096, LANES), f32),
         ),
         in_specs=[vmem(), hbm(), hbm(), hbm(), vmem()],
-        out_specs=(vmem(),) * 7,
+        out_specs=(vmem(),) * 8,
         scratch_shapes=[
             pltpu.VMEM((512, count), jnp.bfloat16),
             pltpu.VMEM((512, count), jnp.bfloat16),
@@ -628,7 +636,7 @@
     )(near(t), far(v), far(wall_film), far(jnp.asarray(smoothing)), owner)
 
 
-def sweeps(v, adv, even, odd, film, smoothing, from_prev, from_next, position):
+def sweeps(v, adv, even, odd, film, smoothing, from_first, from_second, position, cleared):
     f32 = jnp.float32
     bf16 = jnp.bfloat16
     from_even, from_odd, _, _ = gll_tables()
@@ -639,9 +647,9 @@
         out_shape=(
             jax.ShapeDtypeStruct((8, 8, 8, count), f32),
             pltpu.HBM((128, count), f32),
-            jax.ShapeDtypeStruct((4096, LANES), f32),
+            pltpu.VMEM((4096, LANES), f32),
         ),
-        in_specs=[vmem()] * 8 + [hbm()],
+        in_specs=[vmem()] * 8 + [hbm(), vmem()],
         out_specs=(hbm(), hbm(), vmem()),
         scratch_shapes=[
             pltpu.SMEM((16, 128), jnp.int32),
@@ -664,9 +672,10 @@
             pltpu.SemaphoreType.DMA(()),
             pltpu.SemaphoreType.DMA((5,)),
         ],
+        input_output_aliases={9: 2},
         compiler_params=params(28),
         name="sweeps",
-    )(*held, from_prev, from_next, position)
+    )(*held, from_first, from_second, position, near(cleared))
 
 
 def plates(arrived, cell, plate_temp, conductivity):
@@ -737,8 +746,8 @@
     from_first = lax.ppermute(to_first, axes, swaps[0])
     from_second = lax.ppermute(to_second, axes, swaps[1])
     t, v = (x.reshape(8, 8, 8, count) for x in (warmth, velocity))
-    *started, position = begin(t, v, wall_film, face_owner.reshape(16, 128))
-    t_new, wall, sending = sweeps(*started, from_first, from_second, position)
+    *started, position, cleared = begin(t, v, wall_film, face_owner.reshape(16, 128))
+    t_new, wall, sending = sweeps(*started, from_first, from_second, position, cleared)
     cell = plate_cell.reshape(32, LANES)
     arrived = exchange(sending.reshape(128, 32, LANES))
     sheet, returning = plates(arrived, cell, plate_temp, conductivity)

time: 89.6 us -> 89.2 us (level)
  no operation moved by 1% of the time
where the time goes in v4:
time: 89.2 us; the launch traced here: 88.9 us
  blocking collectives  64 us (72%)
  Pallas kernels  17.5 us (20%)
  starting transfers between devices  6.67 us (7%)
    all_to_all x2, blocking collectives, exchange(): return lax.all_to_all(rows, axes, split_axis=0, concat_axis=0, tiled=True)  64 us
    pallas_call x1, Pallas kernels, sweeps(): pl.pallas_call(functools.partial(sweep_kernel, from_even, from_odd), out_...  5.49 us
    ppermute x1, starting transfers between devices, shards(): from_second = lax.ppermute(to_second, axes, swaps[1])  4.55 us
    pallas_call x1, Pallas kernels, begin(): pl.pallas_call(functools.partial(begin_kernel, from_even, from_odd), out_...  3.57 us
    pallas_call x1, Pallas kernels, finish(): pl.pallas_call(finish_kernel, out_shape=(jax.ShapeDtypeStruct((8, 8, 8, c...  3.45 us
    pallas_call x1, Pallas kernels, plates(): pl.pallas_call(owner_kernel, out_shape=(jax.ShapeDtypeStruct((128, 512),...  3.32 us
    ppermute x1, starting transfers between devices, shards(): from_first = lax.ppermute(to_first, axes, swaps[0])  2.12 us
  transfers between devices with their start and end apart: 2, of which 0 were waited for; matrix products, arithmetic and copies ran while one was open for 0% of the time, Pallas kernels for 4%

profile of v4, /device:TPU:1, one launch (start us, length us, event | category | flops | bytes accessed | tf_op | source)
XLA Modules:
  0.0 88.9 jit_solution(1989626340740688627)
XLA Ops:
  0.6 0.0 copy-start
  0.6 0.0 copy-start.2
  0.6 1.7 %edges.1 = (f32[8,512]{1,0:T(8,128)S(1)}, f32[8,512]{1,0:T(8,128)S(1)}) custom-call(f32[512,1024]{1,0:T(8,128)} %t_in.1, f32[512,1024]{1,0:T(8,128)} %v_in.1), custom_call_target="tpu_custom_call" | custom-call | tf_op jit(solution)/shard_map/edges/pallas_call | solution.py:593
  2.4 2.1 %collective-permute-start = (f32[8,512]{1,0:T(8,128)S(1)}, f32[8,512]{1,0:T(8,128)S(1)}, u32[]{:S(2)}, u32[]{:S(2)}) collective-permute-start(f32[8,512]{1,0:T(8,128)S(1)} %get-tuple-element.26), channel_id=1, source_target_pairs={{0,1},{2,3},{4,5},{6,7},{8,9},{10,11},{12,13},{14,15},{16,17},{18,... | collective-permute-start | bytes 49160 | tf_op jit(solution)/shard_map/ppermute | solution.py:746
  4.5 4.6 %collective-permute-start.1 = (f32[8,512]{1,0:T(8,128)S(1)}, f32[8,512]{1,0:T(8,128)S(1)}, u32[]{:S(2)}, u32[]{:S(2)}) collective-permute-start(f32[8,512]{1,0:T(8,128)S(1)} %get-tuple-element.27), channel_id=1, source_target_pairs={{1,2},{3,4},{5,6},{7,8},{9,10},{11,12},{13,14},{15,16},{17,18},{19... | collective-permute-start | bytes 49160 | tf_op jit(solution)/shard_map/ppermute | solution.py:747
  9.1 0.0 copy-done
  9.1 0.0 copy-done.2
  9.1 3.6 %begin.1 = (f32[8,8,8,1024]{3,2,1,0:T(8,128)S(1)}, f32[8,8,8,1024]{3,2,1,0:T(8,128)S(1)}, f32[256,1024]{1,0:T(8,128)S(1)}, f32[256,1024]{1,0:T(8,128)S(1)}, f32[...) custom-call(f32[8,8,8,1024]{3,2,1,0:T(8,128)S(1)} %bitcast.8, ...), custom_call_target="tpu_custom_call" | custom-call | tf_op jit(solution)/shard_map/begin/pallas_call | solution.py:615
  12.7 0.0 collective-permute-done.from_first
  12.7 0.0 collective-permute-done.1.from_second
  12.7 5.5 %sweeps.1 = (f32[8,8,8,1024]{3,2,1,0:T(8,128)}, f32[128,1024]{1,0:T(8,128)}, f32[4096,128]{1,0:T(8,128)S(1)}) custom-call(f32[8,8,8,1024]{3,2,1,0:T(8,128)S(1)} %get-tuple-element.20.v, f32[8,8,8,1024]{3,2,1,0:T(8,128)S(1)} %get-tuple-element.21.adv, f32[256,1024]{1,0:T(8,128)S(1)} %get-tuple-element.22.even_first, ...), custom_call_target="tpu_custom_call", output_to_operand_aliasing={{2}: (9, {})} | custom-call | tf_op jit(solution)/shard_map/sweeps/pallas_call | solution.py:645
  18.2 0.0 copy-start.1
  18.2 41.1 %all_to_all.10.arrived = f32[128,32,128]{2,1,0:T(8,128)S(1)} all-to-all(f32[128,32,128]{2,1,0:T(8,128)S(1)} %bitcast.9), channel_id=1, replica_groups=mesh['flow'=32,'grp'=4] {'flow','grp'}, dimensions={0} | all-to-all | bytes 4194304 | tf_op jit(solution)/shard_map/all_to_all | solution.py:741
  59.2 0.0 copy-done.1
  59.2 3.3 %plates.1 = (f32[128,512]{1,0:T(8,128)}, f32[2048,128]{1,0:T(8,128)S(1)}) custom-call(f32[128,32,128]{2,1,0:T(8,128)S(1)} %all_to_all.10.arrived, s32[32,128]{1,0:T(8,128)S(1)} %bitcast.12, f32[128,512]{1,0:T(8,128)} %plate_in.1, f32[128,512]{1,0:T(8,128)} %conductivity_in.1, bf16[128,256]{1,0:T(8,128)(2,1)} %constant.5.clone.plate_op_in), custom_call_target="tpu_custom_call" | custom-call | tf_op jit(solution)/shard_map/plates/pallas_call | solution.py:684
  62.6 22.9 %all_to_all.11 = f32[128,16,128]{2,1,0:T(8,128)S(1)} all-to-all(f32[128,16,128]{2,1,0:T(8,128)S(1)} %bitcast.11), channel_id=1, replica_groups=mesh['flow'=32,'grp'=4] {'flow','grp'}, dimensions={0} | all-to-all | bytes 2097152 | tf_op jit(solution)/shard_map/all_to_all | solution.py:741
  85.5 3.5 %finish.1 = (f32[8,8,8,1024]{3,2,1,0:T(8,128)}, f32[128,1024]{1,0:T(8,128)}) custom-call(f32[2048,128]{1,0:T(8,128)S(1)} %bitcast.10, s32[16,128]{1,0:T(8,128)S(1)} %get-tuple-element.28.position_in, f32[128,1024]{1,0:T(8,128)} %film_in.3, f32[128,1024]{1,0:T(8,128)} %get-tuple-element.32.wall_in, ...), custom_call_target="tpu_custom_call", output_to_operand_aliasing={{0}: (4, {})} | custom-call | tf_op jit(solution)/shard_map/finish/pallas_call | solution.py:710
Async XLA Ops:
  0.6 8.4 %copy-start = (f32[512,1024]{1,0:T(8,128)S(1)}, f32[512,1024]{1,0:T(8,128)}, u32[]{:S(2)}) copy-start(f32[512,1024]{1,0:T(8,128)} %t_in.1) | copy-start | bytes 6291460
  0.6 8.4 %copy-start.2 = (s32[2048,1]{0,1:T(1,128)S(1)}, s32[2048,1]{0,1:T(1,128)}, u32[]{:S(2)}) copy-start(s32[2048,1]{0,1:T(1,128)} %param.12) | copy-start | bytes 24580
  2.4 10.3 %collective-permute-start = (f32[8,512]{1,0:T(8,128)S(1)}, f32[8,512]{1,0:T(8,128)S(1)}, u32[]{:S(2)}, u32[]{:S(2)}) collective-permute-start(f32[8,512]{1,0:T(8,128)S(1)} %get-tuple-element.26), channel_id=1, source_target_pairs={{0,1},{2,3},{4,5},{6,7},{8,9},{10,11},{12,13},{14,15},{16,17},{18,... | collective-permute-start | bytes 49160 | tf_op jit(solution)/shard_map/ppermute | solution.py:746
  4.5 8.2 %collective-permute-start.1 = (f32[8,512]{1,0:T(8,128)S(1)}, f32[8,512]{1,0:T(8,128)S(1)}, u32[]{:S(2)}, u32[]{:S(2)}) collective-permute-start(f32[8,512]{1,0:T(8,128)S(1)} %get-tuple-element.27), channel_id=1, source_target_pairs={{1,2},{3,4},{5,6},{7,8},{9,10},{11,12},{13,14},{15,16},{17,18},{19... | collective-permute-start | bytes 49160 | tf_op jit(solution)/shard_map/ppermute | solution.py:747
  18.2 41.1 %copy-start.1 = (s32[4096]{0:T(1024)S(1)}, s32[4096]{0:T(1024)}, u32[]{:S(2)}) copy-start(s32[4096]{0:T(1024)} %param.15) | copy-start | bytes 49156

commit v5 on v4

--- a/solution.py
+++ b/solution.py
@@ -197,14 +197,12 @@
     from_odd,
     t,
     v_in,
-    film_in,
     smoothing_in,
     owner,
     v,
     adv,
     even,
     odd,
-    film,
     smoothing,
     position,
     cleared,
@@ -215,7 +213,6 @@
     count = t.shape[-1]
     groups = [[2 * i, 2 * i + 1] for i in range(count // LANES // 2)]
     smoothing_copy = pltpu.make_async_copy(smoothing_in, smoothing, sems.at[0])
-    film_copy = pltpu.make_async_copy(film_in, film, sems.at[1])
     v_copies = []
     for number, group in enumerate(groups):
         lanes = pl.ds(group[0] * LANES, 2 * LANES)
@@ -224,7 +221,7 @@
                 v_in.at[:, :, :, lanes], v.at[:, :, :, lanes], sems.at[2 + number]
             )
         )
-    for copy in [v_copies[0], smoothing_copy] + v_copies[1:] + [film_copy]:
+    for copy in [v_copies[0], smoothing_copy] + v_copies[1:]:
         copy.start()
     cleared[...] = jnp.zeros_like(cleared)
     fill_positions(owner, position)
@@ -254,7 +251,6 @@
         advect(groups[number])
         smooth(smoothing, high, low, even, odd, groups[number - 1])
     smooth(smoothing, high, low, even, odd, groups[-1])
-    film_copy.wait()
 
 
 def sweep_kernel(
@@ -264,7 +260,7 @@
     adv,
     even_first,
     odd_first,
-    film,
+    film_in,
     smoothing,
     from_first,
     from_second,
@@ -274,6 +270,7 @@
     wall_out,
     sending,
     position,
+    film,
     wall,
     t_edge,
     v_edge,
@@ -296,6 +293,8 @@
     del cleared
     position_copy = pltpu.make_async_copy(position_in, position, in_sem)
     position_copy.start()
+    film_copy = pltpu.make_async_copy(film_in, film, out_sems.at[5])
+    film_copy.start()
     count = v.shape[-1]
     inner = count // LANES
     blocks = inner + 1
@@ -395,6 +394,7 @@
     carry_inner(groups[0])
     carry_edge(1, functools.partial(combine, 0, adv_edge.at[0], block=inner))
     position_copy.wait()
+    film_copy.wait()
     smooth(smoothing, high, low, even_second, odd_second, groups[0])
     for number in range(1, len(groups)):
         carry_inner(groups[number])
@@ -608,7 +608,7 @@
     return pltpu.with_memory_space_constraint(array, pltpu.VMEM)
 
 
-def begin(t, v, wall_film, owner):
+def begin(t, v, owner):
     f32 = jnp.float32
     from_even, from_odd, smoothing, _ = gll_tables()
     count = t.shape[-1]
@@ -619,13 +619,12 @@
             pltpu.VMEM((8, 8, 8, count), f32),
             pltpu.VMEM((256, count), f32),
             pltpu.VMEM((256, count), f32),
-            pltpu.VMEM((128, count), f32),
             pltpu.VMEM((2, 256, 512), jnp.bfloat16),
             jax.ShapeDtypeStruct((16, 128), jnp.int32),
             pltpu.VMEM((4096, LANES), f32),
         ),
-        in_specs=[vmem(), hbm(), hbm(), hbm(), vmem()],
-        out_specs=(vmem(),) * 8,
+        in_specs=[vmem(), hbm(), hbm(), vmem()],
+        out_specs=(vmem(),) * 7,
         scratch_shapes=[
             pltpu.VMEM((512, count), jnp.bfloat16),
             pltpu.VMEM((512, count), jnp.bfloat16),
@@ -633,7 +632,7 @@
         ],
         compiler_params=params(20),
         name="begin",
-    )(near(t), far(v), far(wall_film), far(jnp.asarray(smoothing)), owner)
+    )(near(t), far(v), far(jnp.asarray(smoothing)), owner)
 
 
 def sweeps(v, adv, even, odd, film, smoothing, from_first, from_second, position, cleared):
@@ -641,7 +640,7 @@
     bf16 = jnp.bfloat16
     from_even, from_odd, _, _ = gll_tables()
     count = v.shape[-1]
-    held = [near(x) for x in (v, adv, even, odd, film, smoothing)]
+    held = [near(x) for x in (v, adv, even, odd)] + [far(film), near(smoothing)]
     return pl.pallas_call(
         functools.partial(sweep_kernel, from_even, from_odd),
         out_shape=(
@@ -649,10 +648,11 @@
             pltpu.HBM((128, count), f32),
             pltpu.VMEM((4096, LANES), f32),
         ),
-        in_specs=[vmem()] * 8 + [hbm(), vmem()],
+        in_specs=[vmem()] * 4 + [hbm()] + [vmem()] * 3 + [hbm(), vmem()],
         out_specs=(hbm(), hbm(), vmem()),
         scratch_shapes=[
             pltpu.SMEM((16, 128), jnp.int32),
+            pltpu.VMEM((128, count), f32),
             pltpu.VMEM((128, count), f32),
             pltpu.VMEM((8, 8, 8, LANES), f32),
             pltpu.VMEM((8, 8, 8, LANES), f32),
@@ -670,7 +670,7 @@
             pltpu.VMEM((128, 512), f32),
             pltpu.VMEM((2, count, LANES), f32),
             pltpu.SemaphoreType.DMA(()),
-            pltpu.SemaphoreType.DMA((5,)),
+            pltpu.SemaphoreType.DMA((6,)),
         ],
         input_output_aliases={9: 2},
         compiler_params=params(28),
@@ -746,8 +746,10 @@
     from_first = lax.ppermute(to_first, axes, swaps[0])
     from_second = lax.ppermute(to_second, axes, swaps[1])
     t, v = (x.reshape(8, 8, 8, count) for x in (warmth, velocity))
-    *started, position, cleared = begin(t, v, wall_film, face_owner.reshape(16, 128))
-    t_new, wall, sending = sweeps(*started, from_first, from_second, position, cleared)
+    *started, smoothing, position, cleared = begin(t, v, face_owner.reshape(16, 128))
+    t_new, wall, sending = sweeps(
+        *started, wall_film, smoothing, from_first, from_second, position, cleared
+    )
     cell = plate_cell.reshape(32, LANES)
     arrived = exchange(sending.reshape(128, 32, LANES))
     sheet, returning = plates(arrived, cell, plate_temp, conductivity)

time: 89.2 us -> 89.3 us (level)
  no operation moved by 1% of the time
where the time goes in v5:
time: 89.3 us; the launch traced here: 89 us
  blocking collectives  64 us (72%)
  Pallas kernels  17.6 us (20%)
  starting transfers between devices  6.67 us (7%)
    all_to_all x2, blocking collectives, exchange(): return lax.all_to_all(rows, axes, split_axis=0, concat_axis=0, tiled=True)  64 us
    pallas_call x1, Pallas kernels, sweeps(): pl.pallas_call(functools.partial(sweep_kernel, from_even, from_odd), out_...  5.55 us
    ppermute x1, starting transfers between devices, shards(): from_second = lax.ppermute(to_second, axes, swaps[1])  4.55 us
    pallas_call x1, Pallas kernels, begin(): pl.pallas_call(functools.partial(begin_kernel, from_even, from_odd), out_...  3.56 us
    pallas_call x1, Pallas kernels, finish(): pl.pallas_call(finish_kernel, out_shape=(jax.ShapeDtypeStruct((8, 8, 8, c...  3.45 us
    pallas_call x1, Pallas kernels, plates(): pl.pallas_call(owner_kernel, out_shape=(jax.ShapeDtypeStruct((128, 512),...  3.32 us
    ppermute x1, starting transfers between devices, shards(): from_first = lax.ppermute(to_first, axes, swaps[0])  2.12 us
  transfers between devices with their start and end apart: 2, of which 0 were waited for; matrix products, arithmetic and copies ran while one was open for 0% of the time, Pallas kernels for 4%

profile of v5, /device:TPU:1, one launch (start us, length us, event | category | flops | bytes accessed | tf_op | source)
XLA Modules:
  0.0 89.0 jit_solution(11739164014256243166)
XLA Ops:
  0.6 0.0 copy-start
  0.6 0.0 copy-start.2
  0.6 1.7 %edges.1 = (f32[8,512]{1,0:T(8,128)S(1)}, f32[8,512]{1,0:T(8,128)S(1)}) custom-call(f32[512,1024]{1,0:T(8,128)} %t_in.1, f32[512,1024]{1,0:T(8,128)} %v_in.1), custom_call_target="tpu_custom_call" | custom-call | tf_op jit(solution)/shard_map/edges/pallas_call | solution.py:593
  2.4 2.1 %collective-permute-start = (f32[8,512]{1,0:T(8,128)S(1)}, f32[8,512]{1,0:T(8,128)S(1)}, u32[]{:S(2)}, u32[]{:S(2)}) collective-permute-start(f32[8,512]{1,0:T(8,128)S(1)} %get-tuple-element.24), channel_id=1, source_target_pairs={{0,1},{2,3},{4,5},{6,7},{8,9},{10,11},{12,13},{14,15},{16,17},{18,... | collective-permute-start | bytes 49160 | tf_op jit(solution)/shard_map/ppermute | solution.py:746
  4.5 4.6 %collective-permute-start.1 = (f32[8,512]{1,0:T(8,128)S(1)}, f32[8,512]{1,0:T(8,128)S(1)}, u32[]{:S(2)}, u32[]{:S(2)}) collective-permute-start(f32[8,512]{1,0:T(8,128)S(1)} %get-tuple-element.25), channel_id=1, source_target_pairs={{1,2},{3,4},{5,6},{7,8},{9,10},{11,12},{13,14},{15,16},{17,18},{19... | collective-permute-start | bytes 49160 | tf_op jit(solution)/shard_map/ppermute | solution.py:747
  9.1 0.0 copy-done
  9.1 0.0 copy-done.2
  9.1 3.6 %begin.1 = (f32[8,8,8,1024]{3,2,1,0:T(8,128)S(1)}, f32[8,8,8,1024]{3,2,1,0:T(8,128)S(1)}, f32[256,1024]{1,0:T(8,128)S(1)}, f32[256,1024]{1,0:T(8,128)S(1)}, bf16...) custom-call(f32[8,8,8,1024]{3,2,1,0:T(8,128)S(1)} %bitcast.8, ...), custom_call_target="tpu_custom_call" | custom-call | tf_op jit(solution)/shard_map/begin/pallas_call | solution.py:615
  12.6 0.0 collective-permute-done.from_first
  12.7 0.0 collective-permute-done.1.from_second
  12.7 5.5 %sweeps.1 = (f32[8,8,8,1024]{3,2,1,0:T(8,128)}, f32[128,1024]{1,0:T(8,128)}, f32[4096,128]{1,0:T(8,128)S(1)}) custom-call(f32[8,8,8,1024]{3,2,1,0:T(8,128)S(1)} %get-tuple-element.19.v, f32[8,8,8,1024]{3,2,1,0:T(8,128)S(1)} %get-tuple-element.20.adv, f32[256,1024]{1,0:T(8,128)S(1)} %get-tuple-element.21.even_first, ...), custom_call_target="tpu_custom_call", output_to_operand_aliasing={{2}: (9, {})} | custom-call | tf_op jit(solution)/shard_map/sweeps/pallas_call | solution.py:644
  18.2 0.0 copy-start.1
  18.2 41.1 %all_to_all.10.arrived = f32[128,32,128]{2,1,0:T(8,128)S(1)} all-to-all(f32[128,32,128]{2,1,0:T(8,128)S(1)} %bitcast.9), channel_id=1, replica_groups=mesh['flow'=32,'grp'=4] {'flow','grp'}, dimensions={0} | all-to-all | bytes 4194304 | tf_op jit(solution)/shard_map/all_to_all | solution.py:741
  59.3 0.0 copy-done.1
  59.3 3.3 %plates.1 = (f32[128,512]{1,0:T(8,128)}, f32[2048,128]{1,0:T(8,128)S(1)}) custom-call(f32[128,32,128]{2,1,0:T(8,128)S(1)} %all_to_all.10.arrived, s32[32,128]{1,0:T(8,128)S(1)} %bitcast.12, f32[128,512]{1,0:T(8,128)} %plate_in.1, f32[128,512]{1,0:T(8,128)} %conductivity_in.1, bf16[128,256]{1,0:T(8,128)(2,1)} %constant.5.clone.plate_op_in), custom_call_target="tpu_custom_call" | custom-call | tf_op jit(solution)/shard_map/plates/pallas_call | solution.py:684
  62.6 22.9 %all_to_all.11 = f32[128,16,128]{2,1,0:T(8,128)S(1)} all-to-all(f32[128,16,128]{2,1,0:T(8,128)S(1)} %bitcast.11), channel_id=1, replica_groups=mesh['flow'=32,'grp'=4] {'flow','grp'}, dimensions={0} | all-to-all | bytes 2097152 | tf_op jit(solution)/shard_map/all_to_all | solution.py:741
  85.5 3.5 %finish.1 = (f32[8,8,8,1024]{3,2,1,0:T(8,128)}, f32[128,1024]{1,0:T(8,128)}) custom-call(f32[2048,128]{1,0:T(8,128)S(1)} %bitcast.10, s32[16,128]{1,0:T(8,128)S(1)} %get-tuple-element.26.position_in, f32[128,1024]{1,0:T(8,128)} %film_in.3, f32[128,1024]{1,0:T(8,128)} %get-tuple-element.30.wall_in, ...), custom_call_target="tpu_custom_call", output_to_operand_aliasing={{0}: (4, {})} | custom-call | tf_op jit(solution)/shard_map/finish/pallas_call | solution.py:710
Async XLA Ops:
  0.6 8.4 %copy-start = (f32[512,1024]{1,0:T(8,128)S(1)}, f32[512,1024]{1,0:T(8,128)}, u32[]{:S(2)}) copy-start(f32[512,1024]{1,0:T(8,128)} %t_in.1) | copy-start | bytes 6291460
  0.6 8.4 %copy-start.2 = (s32[2048,1]{0,1:T(1,128)S(1)}, s32[2048,1]{0,1:T(1,128)}, u32[]{:S(2)}) copy-start(s32[2048,1]{0,1:T(1,128)} %param.12) | copy-start | bytes 24580
  2.4 10.3 %collective-permute-start = (f32[8,512]{1,0:T(8,128)S(1)}, f32[8,512]{1,0:T(8,128)S(1)}, u32[]{:S(2)}, u32[]{:S(2)}) collective-permute-start(f32[8,512]{1,0:T(8,128)S(1)} %get-tuple-element.24), channel_id=1, source_target_pairs={{0,1},{2,3},{4,5},{6,7},{8,9},{10,11},{12,13},{14,15},{16,17},{18,... | collective-permute-start | bytes 49160 | tf_op jit(solution)/shard_map/ppermute | solution.py:746
  4.5 8.2 %collective-permute-start.1 = (f32[8,512]{1,0:T(8,128)S(1)}, f32[8,512]{1,0:T(8,128)S(1)}, u32[]{:S(2)}, u32[]{:S(2)}) collective-permute-start(f32[8,512]{1,0:T(8,128)S(1)} %get-tuple-element.25), channel_id=1, source_target_pairs={{1,2},{3,4},{5,6},{7,8},{9,10},{11,12},{13,14},{15,16},{17,18},{19... | collective-permute-start | bytes 49160 | tf_op jit(solution)/shard_map/ppermute | solution.py:747
  18.2 41.1 %copy-start.1 = (s32[4096]{0:T(1024)S(1)}, s32[4096]{0:T(1024)}, u32[]{:S(2)}) copy-start(s32[4096]{0:T(1024)} %param.15) | copy-start | bytes 49156
